TPU v7x, 512 devices: a whole 4x8x8 slice. The times are simulated.
512 devices in a mesh: stream: 16 (over z_hi, x), span: 32 (over z_lo, y, core).
Axes of the slice: x: 4, y: 8, z: 8 (z_hi: 4, z_lo: 2; z = z_hi * 2 + z_lo), core: 2. Of those that a mesh axis runs over, the one named last changes fastest.
Arguments:
- fine_pops: float32 [27, 96, 192, 128], P(None, 'stream', 'span'), may hold values from 0.5 to 2
- coarse_pops: float32 [27, 48, 96, 64], P(None, 'stream', 'span'), may hold values from 0.5 to 2
- obstacle: int32 [96, 192, 128], P('stream', 'span'), may hold values from 0 to 1, as said below
- block_level: int32 [16, 32], replicated, may hold values 0 or 1
- relax_rates: float32 [27], replicated, may hold values from 0.5 to 1.9
Outputs:
- fine_next: float32 [27, 96, 192, 128], P(None, 'stream', 'span')
- coarse_next: float32 [27, 48, 96, 64], P(None, 'stream', 'span')
Inputs may be any that keep to these rules, and one draw needn't show every extreme that they name: `block_level`: 1 marks a refined block, whose fine cells are active; 0 a coarse block. `obstacle`: 1 marks a building cell. No building cell has a first index x with x % 6 below 2 or at least 4, nor a second index y with y % 6 below 2 or at least 4; a building cell stands on the ground or on another building cell.
All inputs are finite; a program needn't handle non-finite values.
Results may differ from a plain program's by a relative error of at most 0.0003.
Values sent between devices are 32-bit elements; how exact they have to be, the bound alone decides.
A program may use at most 64 MiB of HBM per device.

v0:
```python
import functools

import jax
import jax.numpy as jnp
from jax import lax
from jax.experimental import pallas as pl
from jax.experimental.pallas import tpu as pltpu
from jax.sharding import PartitionSpec as P

MESH = pl.DeviceIdType.MESH
F32 = jnp.float32
FACES = ((-1, 0), (1, 0), (0, -1), (0, 1))
CORNERS = ((-1, -1), (-1, 1), (1, -1), (1, 1))


def face_pops(side):
    dx, dy = side
    return [q for q in range(27) if (q // 9 - 1 == -dx if dx else q // 3 % 3 - 1 == -dy)]


def corner_start(side):
    dx, dy = side
    return 9 * (1 - dx) + 3 * (1 - dy)


def face_cells(side):
    dx, dy = side
    return [(1 - dx, j) for j in range(3)] if dx else [(i, 1 - dy) for i in range(3)]


def end_pops(side):
    dx, dy = side
    return [face_pops((0, s) if dx else (s, 0)) for s in (-1, 1)]


def pick_rows(cell, pops):
    return jnp.concatenate([cell[q : q + 3] for q in pops[::3]], axis=0)


def exchange_kernel(
    n_stream, n_span, fine, coarse, level, turned, faces, corners, own,
    native, levels, face_out, corner_out, load_sem, send_sem, recv_sem,
):
    row, col = lax.axis_index("stream"), lax.axis_index("span")

    def at(side):
        return (lax.rem(row + side[0] + n_stream, n_stream), lax.rem(col + side[1] + n_span, n_span))

    barrier = pltpu.get_barrier_semaphore()
    for side in CORNERS + FACES:
        pl.semaphore_signal(barrier, inc=1, device_id=at(side), device_id_type=MESH)
    loads = [
        pltpu.make_async_copy(fine, native, load_sem.at[0]),
        pltpu.make_async_copy(coarse, own, load_sem.at[1]),
        pltpu.make_async_copy(level, levels, load_sem.at[2]),
    ]
    for load in loads:
        load.start()
    for load in loads:
        load.wait()
    here = levels[row, col]
    for x in range(6):
        turned[:, x + 1, pl.ds(1, 6), :] = jnp.swapaxes(native[x], 0, 1)
    for slot, side in enumerate(FACES):
        dx, dy = side
        to = at((-dx, -dy))
        both = (here == 1) & (levels[to[0], to[1]] == 1)
        cells = [own[i, j] for i, j in face_cells(side)]
        pair = jnp.concatenate([cells[0], cells[1]], axis=1)
        last = jnp.concatenate([cells[2], cells[2]], axis=1)
        blocks = jnp.concatenate([pair, last], axis=0)
        if dx:
            rows = [turned[q, 6 if dx < 0 else 1, pl.ds(1, 6), :] for q in face_pops(side)]
        else:
            rows = [turned[q, pl.ds(1, 6), 6 if dy < 0 else 1, :] for q in face_pops(side)]
        strips = jnp.concatenate(rows, axis=0)
        face_out[slot, pl.ds(0, 54), :] = jnp.where(both, strips, blocks)
        ends = [pick_rows(cell, pops) for cell, pops in zip((cells[0], cells[2]), end_pops(side))]
        face_out[slot, pl.ds(54, 9), :] = jnp.concatenate(ends, axis=1)
    for slot, side in enumerate(CORNERS):
        dx, dy = side
        cell = own[1 - dx, 1 - dy]
        corner_out[slot, pl.ds(0, 14), :] = jnp.concatenate([cell[0:14], cell[13:27]], axis=1)
        corner_out[slot, pl.ds(14, 3), :] = native[
            5 if dx < 0 else 0, 5 if dy < 0 else 0, pl.ds(corner_start(side), 3), :
        ]
    pl.semaphore_wait(barrier, 8)
    copies = []
    for slot, (dx, dy) in enumerate(FACES):
        copies.append(
            pltpu.make_async_remote_copy(
                face_out.at[slot, pl.ds(0, 63)], faces.at[slot, pl.ds(0, 63)],
                send_sem.at[slot], recv_sem.at[slot], device_id=at((-dx, -dy)), device_id_type=MESH,
            )
        )
    for slot, (dx, dy) in enumerate(CORNERS):
        copies.append(
            pltpu.make_async_remote_copy(
                corner_out.at[slot, pl.ds(0, 17)], corners.at[slot, pl.ds(0, 17)],
                send_sem.at[4 + slot], recv_sem.at[4 + slot], device_id=at((-dx, -dy)), device_id_type=MESH,
            )
        )
    for copy in copies:
        copy.start()
    for copy in copies:
        copy.wait()


def exchange(n_stream, n_span, fine, coarse, level):
    anywhere = pl.BlockSpec(memory_space=pl.ANY)
    vmem = pl.BlockSpec(memory_space=pltpu.VMEM)
    return pl.pallas_call(
        functools.partial(exchange_kernel, n_stream, n_span),
        out_shape=(
            jax.ShapeDtypeStruct((27, 8, 8, 128), F32),
            jax.ShapeDtypeStruct((4, 64, 128), F32),
            jax.ShapeDtypeStruct((4, 24, 128), F32),
            jax.ShapeDtypeStruct((3, 3, 27, 64), F32),
        ),
        in_specs=[anywhere] * 3,
        out_specs=(vmem,) * 4,
        scratch_shapes=[
            pltpu.VMEM((6, 6, 27, 128), F32),
            pltpu.SMEM((16, 32), jnp.int32),
            pltpu.VMEM((4, 64, 128), F32),
            pltpu.VMEM((4, 24, 128), F32),
            pltpu.SemaphoreType.DMA((3,)),
            pltpu.SemaphoreType.DMA((8,)),
            pltpu.SemaphoreType.DMA((8,)),
        ],
        compiler_params=pltpu.CompilerParams(
            collective_id=0, has_side_effects=True, vmem_limit_bytes=24 * 2**20
        ),
    )(fine, coarse, level)


def scalars(rates, coarse):
    keep, pull = [], {}
    for q in range(27):
        rate = rates[q]
        if coarse:
            rate = 1.0 / (2.0 / rate - 0.5)
        keep.append((1.0 - rate) * 0.125)
        orders = (q // 9, q // 3 % 3, q % 3)
        if 1 not in orders:
            pull[q] = rate * (0.125 / 3.0 ** orders.count(2))
    return keep, pull


def forward(low, mid, high, speed, total=None):
    pair, diff = high + low, high - low
    if total is None:
        total = pair + 4.0 * mid
    first = diff - speed * total
    return total, first, pair - speed * (diff + first)


def backward(total, first, second, speed):
    slope = first + speed * total
    curve = second + speed * (first + slope)
    return curve - slope, 0.5 * (total - curve), curve + slope


def collide(g, keep, pull):
    t0 = [g[r] + g[18 + r] + 4.0 * g[9 + r] for r in range(9)]
    dx = [g[18 + r] - g[r] for r in range(9)]
    s0 = [t0[c] + t0[6 + c] + 4.0 * t0[3 + c] for c in range(3)]
    dy = [t0[6 + c] - t0[c] for c in range(3)]
    density = s0[0] + s0[2] + 4.0 * s0[1]
    ex = [dx[c] + dx[6 + c] + 4.0 * dx[3 + c] for c in range(3)]
    inverse = 1.0 / density
    ux = (ex[0] + ex[2] + 4.0 * ex[1]) * inverse
    uy = (dy[0] + dy[2] + 4.0 * dy[1]) * inverse
    uz = (s0[2] - s0[0]) * inverse
    k = [None] * 27
    for r in range(9):
        k[r], k[9 + r], k[18 + r] = forward(g[r], g[9 + r], g[18 + r], ux, t0[r])
    for a in range(3):
        for c in range(3):
            i = 9 * a + c
            k[i], k[i + 3], k[i + 6] = forward(k[i], k[i + 3], k[i + 6], uy, s0[c] if a == 0 else None)
    for i in range(0, 27, 3):
        k[i], k[i + 1], k[i + 2] = forward(k[i], k[i + 1], k[i + 2], uz, density if i == 0 else None)
    for q in range(27):
        k[q] = keep[q] * k[q] + pull[q] * density if q in pull else keep[q] * k[q]
    for i in range(0, 27, 3):
        k[i], k[i + 1], k[i + 2] = backward(k[i], k[i + 1], k[i + 2], uz)
    for a in range(3):
        for c in range(3):
            i = 9 * a + c
            k[i], k[i + 3], k[i + 6] = backward(k[i], k[i + 3], k[i + 6], uy)
    for r in range(9):
        k[r], k[9 + r], k[18 + r] = backward(k[r], k[9 + r], k[18 + r], ux)
    return k


def lane(shape):
    return lax.broadcasted_iota(jnp.int32, shape, len(shape) - 1)


def take(values, index):
    return jnp.take_along_axis(values, index, axis=1)


def stretch(values):
    at = lane(values.shape)
    middle = lax.shift_right_logical(at, 1)
    beside = jnp.clip(middle + 2 * (at & 1) - 1, 0, 63)
    return 0.75 * take(values, middle) + 0.25 * take(values, beside)


def shrink(values):
    at = lane(values.shape)
    even = jnp.minimum(2 * at, 126)
    return (take(values, even) + take(values, even + 1)) * 0.125


def mix(near, far):
    return 0.75 * near + 0.25 * far


def step_kernel(
    n_stream, n_span, given, faces, corners, own, obstacle, levels, rates, fine_out, coarse_out, turned,
    halo, tall, blocked, rolled, coarse_blocked,
):
    row, col = lax.axis_index("stream"), lax.axis_index("span")

    def level_at(side):
        return levels[
            lax.rem(row + side[0] + n_stream, n_stream), lax.rem(col + side[1] + n_span, n_span)
        ]

    refined = levels[row, col] == 1

    for i in range(3):
        for j in range(3):
            halo[i + 1, j + 1, pl.ds(0, 27), pl.ds(0, 64)] = own[i, j]
    for slot, (dx, dy) in enumerate(CORNERS):
        both = corners[slot, pl.ds(0, 14), :]
        cell = halo.at[2 + 2 * dx, 2 + 2 * dy]
        cell[pl.ds(13, 14), :] = pltpu.roll(both, 64, 1)
        cell[pl.ds(0, 14), :] = both
    for slot, side in enumerate(FACES):
        dx, dy = side
        spots = [(2 + 2 * dx, 1 + j) if dx else (1 + j, 2 + 2 * dy) for j in range(3)]
        plain = (levels[row, col] == 0) | (level_at(side) == 0)

        @pl.when(plain)
        def _():
            pair = faces[slot, pl.ds(0, 27), :]
            halo[spots[0][0], spots[0][1], pl.ds(0, 27), :] = pair
            halo[spots[1][0], spots[1][1], pl.ds(0, 27), :] = pltpu.roll(pair, 64, 1)
            halo[spots[2][0], spots[2][1], pl.ds(0, 27), :] = faces[slot, pl.ds(27, 27), :]

        @pl.when(jnp.logical_not(plain))
        def _():
            ends = faces[slot, pl.ds(54, 9), :]
            for spot, pops, rows in zip((spots[0], spots[2]), end_pops(side), (ends, pltpu.roll(ends, 64, 1))):
                for n in (0, 3, 6):
                    halo[spot[0], spot[1], pl.ds(pops[n], 3), :] = rows[n : n + 3]

    for i in range(5):
        for j in range(5):
            tall[i, j, pl.ds(0, 27), :] = stretch(halo[i, j, pl.ds(0, 27), :])

    def tall_at(i, j, start, count):
        return tall[i, j, pl.ds(start, count), :]

    @pl.when(refined)
    def _():
        keep, pull = scalars(rates, False)
        for slot, side in enumerate(FACES):
            dx, dy = side
            pops = face_pops(side)
            edge, inner = 2 + 2 * (dx + dy), 2 + (dx + dy)
            rim = 7 if dx + dy > 0 else 0

            def store(n, q, values):
                if dx:
                    turned[q, rim, pl.ds(1, 6), :] = values
                else:
                    turned[q, pl.ds(1, 6), rim, :] = values

            @pl.when(level_at(side) == 1)
            def _():
                for n, q in enumerate(pops):
                    store(n, q, faces[slot, pl.ds(6 * n, 6), :])

            @pl.when(level_at(side) == 0)
            def _():
                first, count = (pops[0], 9) if dx else (0, 27)
                if dx:
                    line = [mix(tall_at(edge, j, first, count), tall_at(inner, j, first, count)) for j in range(5)]
                else:
                    line = [mix(tall_at(i, edge, first, count), tall_at(i, inner, first, count)) for i in range(5)]
                cells = []
                for n in range(6):
                    cells.append(mix(line[n // 2 + 1], line[n // 2 + 2 * (n % 2)]))
                turn = jnp.swapaxes(jnp.stack(cells), 0, 1)
                for n, q in enumerate(pops):
                    store(n, q, turn[q - first])

        for slot, side in enumerate(CORNERS):
            dx, dy = side
            start = corner_start(side)
            ei, ii, ej, ij = 2 + 2 * dx, 2 + dx, 2 + 2 * dy, 2 + dy
            exploded = mix(
                mix(tall_at(ei, ej, start, 3), tall_at(ii, ej, start, 3)),
                mix(tall_at(ei, ij, start, 3), tall_at(ii, ij, start, 3)),
            )
            value = jnp.where(level_at(side) == 1, corners[slot, pl.ds(14, 3), :], exploded)
            for c in range(3):
                turned[start + c, 7 if dx > 0 else 0, pl.ds(7 if dy > 0 else 0, 1), :] = value[c : c + 1]

        blocked[...] = jnp.zeros_like(blocked)
        blocked[pl.ds(1, 6), pl.ds(1, 6), :] = obstacle[...]
        at = lane((8, 128))
        for x in range(8):
            flags = blocked[x]
            rolled[1, x] = flags
            rolled[2, x] = jnp.where(at == 0, 1, pltpu.roll(flags, 1, 1))
            rolled[0, x] = jnp.where(at == 127, 1, pltpu.roll(flags, 127, 1))

        def line(x, carry):
            g, mid = [], []
            for q in range(27):
                ex, ey, ez = q // 9 - 1, q // 3 % 3 - 1, q % 3 - 1
                source = turned[q, x + 1 - ex, pl.ds(1 - ey, 6), :]
                if ez:
                    source = pltpu.roll(source, ez % 128, 1)
                if q == 13:
                    g.append(source)
                    continue
                stop = rolled[ez + 1, x + 1 - ex, pl.ds(1 - ey, 6), :]
                g.append(jnp.where(stop != 0, turned[26 - q, x + 1, pl.ds(1, 6), :], source))
            new = collide(g, keep, pull)
            wall = blocked[x + 1, pl.ds(1, 6), :] != 0
            new = [jnp.where(wall, turned[q, x + 1, pl.ds(1, 6), :], new[q]) for q in range(27)]
            fine_out[x] = jnp.swapaxes(jnp.stack(new), 0, 1)
            return carry

        lax.fori_loop(0, 6, line, 0)
        for i in range(3):
            for j in range(3):
                total = (fine_out[2 * i, 2 * j] + fine_out[2 * i, 2 * j + 1]) + (
                    fine_out[2 * i + 1, 2 * j] + fine_out[2 * i + 1, 2 * j + 1]
                )
                coarse_out[i, j] = shrink(total)[:, :64]

    @pl.when(jnp.logical_not(refined))
    def _():
        for x in range(6):
            line = [
                mix(tall_at(x // 2 + 1, j, 0, 27), tall_at(x // 2 + 2 * (x % 2), j, 0, 27)) for j in range(5)
            ]
            for y in range(6):
                fine_out[x, y] = mix(line[y // 2 + 1], line[y // 2 + 2 * (y % 2)])

        keep, pull = scalars(rates, True)
        flat = turned.reshape(27 * 64, 128)
        for i in range(5):
            cells = jnp.swapaxes(halo[i, :, pl.ds(0, 27), :], 0, 1)
            for q in range(27):
                flat[pl.ds(64 * q + 5 * i, 5), :] = cells[q]
        column = jnp.maximum(
            jnp.maximum(obstacle[2, pl.ds(2, 1), :], obstacle[2, pl.ds(3, 1), :]),
            jnp.maximum(obstacle[3, pl.ds(2, 1), :], obstacle[3, pl.ds(3, 1), :]),
        )
        at = lane((1, 128))
        even = jnp.minimum(2 * at, 126)
        wide = jnp.broadcast_to(column, (8, 128))
        even = jnp.broadcast_to(even, (8, 128))
        flags = jnp.maximum(take(wide, even), take(wide, even + 1))[:1]
        flags = jnp.where(at < 64, flags, 0)
        coarse_blocked[...] = jnp.zeros_like(coarse_blocked)
        coarse_blocked[1, pl.ds(12, 1), :] = flags
        high = lane((32, 128))
        coarse_blocked[2] = jnp.where(high == 0, 1, pltpu.roll(coarse_blocked[1], 1, 1))
        coarse_blocked[0] = jnp.where(high == 63, 1, pltpu.roll(coarse_blocked[1], 127, 1))
        g = []
        for q in range(27):
            ex, ey, ez = q // 9 - 1, q // 3 % 3 - 1, q % 3 - 1
            start = 6 - 5 * ex - ey
            source = flat[pl.ds(64 * q + start, 13), :]
            if ez:
                source = pltpu.roll(source, ez % 128, 1)
            if q != 13:
                stop = coarse_blocked[ez + 1, pl.ds(start, 13), :]
                source = jnp.where(stop != 0, flat[pl.ds(64 * (26 - q) + 6, 13), :], source)
            g.append(source)
        new = collide(g, keep, pull)
        wall = coarse_blocked[1, pl.ds(6, 13), :] != 0
        new = [jnp.where(wall, flat[pl.ds(64 * q + 6, 13), :], new[q]) for q in range(27)]
        turn = jnp.swapaxes(jnp.stack(new), 0, 1)
        for i in range(3):
            for j in range(3):
                coarse_out[i, j] = turn[5 * i + j][:, :64]


def step(n_stream, n_span, turned, faces, corners, own, obstacle, level, rates):
    vmem = pl.BlockSpec(memory_space=pltpu.VMEM)
    smem = pl.BlockSpec(memory_space=pltpu.SMEM)
    return pl.pallas_call(
        functools.partial(step_kernel, n_stream, n_span),
        out_shape=(
            jax.ShapeDtypeStruct((6, 6, 27, 128), F32),
            jax.ShapeDtypeStruct((3, 3, 27, 64), F32),
            jax.ShapeDtypeStruct((27, 8, 8, 128), F32),
        ),
        in_specs=[vmem] * 5 + [smem] * 2,
        out_specs=(vmem,) * 3,
        input_output_aliases={0: 2},
        scratch_shapes=[
            pltpu.VMEM((5, 5, 32, 128), F32),
            pltpu.VMEM((5, 5, 32, 128), F32),
            pltpu.VMEM((8, 8, 128), jnp.int32),
            pltpu.VMEM((3, 8, 8, 128), jnp.int32),
            pltpu.VMEM((3, 32, 128), jnp.int32),
        ],
        compiler_params=pltpu.CompilerParams(vmem_limit_bytes=24 * 2**20),
    )(turned, faces, corners, own, obstacle, level, rates)


def solution(mesh):
    n_stream, n_span = mesh.shape["stream"], mesh.shape["span"]

    def local(fine_pops, coarse_pops, obstacle, block_level, relax_rates):
        fine = jnp.transpose(fine_pops, (1, 2, 0, 3))
        coarse = jnp.transpose(coarse_pops, (1, 2, 0, 3))
        turned, faces, corners, own = exchange(n_stream, n_span, fine, coarse, block_level)
        fine_next, coarse_next, _ = step(
            n_stream, n_span, turned, faces, corners, own, obstacle, block_level, relax_rates
        )
        return jnp.transpose(fine_next, (2, 0, 1, 3)), jnp.transpose(coarse_next, (2, 0, 1, 3))

    placed = P(None, "stream", "span", None)
    return jax.shard_map(
        local,
        mesh=mesh,
        in_specs=(placed, placed, P("stream", "span", None), P(), P()),
        out_specs=(placed, placed),
        check_vma=False,
    )
```

profile of v0, /device:TPU:1, one launch (start us, length us, event | category | flops | bytes accessed | tf_op | source)
XLA Modules:
  0.0 27.7 jit_solution(971634802145896398)
XLA Ops:
  0.6 0.0 copy-start
  0.6 1.1 %copy-done = f32[27,6,6,128]{3,0,2,1:T(8,128)S(1)} copy-done((f32[27,6,6,128]{3,0,2,1:T(8,128)S(1)}, f32[27,6,6,128]{3,0,2,1:T(8,128)}, u32[]{:S(2)}) %copy-start) | copy-done | bytes 497688
  1.7 0.0 copy-start.1
  1.7 0.9 %copy-done.1 = f32[27,3,3,64]{3,0,2,1:T(8,128)S(1)} copy-done((f32[27,3,3,64]{3,0,2,1:T(8,128)S(1)}, f32[27,3,3,64]{3,0,2,1:T(8,128)}, u32[]{:S(2)}) %copy-start.1) | copy-done | bytes 62232
  2.6 0.0 copy-start.2
  2.6 0.7 %copy-done.2 = s32[16,32]{1,0:T(8,128)S(1)} copy-done((s32[16,32]{1,0:T(8,128)S(1)}, s32[16,32]{1,0:T(8,128)}, u32[]{:S(2)}) %copy-start.2) | copy-done | bytes 2072
  3.3 0.0 copy-start.3
  3.3 19.9 %shard_map.68 = (f32[27,8,8,128]{3,2,1,0:T(8,128)S(1)}, f32[4,64,128]{2,1,0:T(8,128)S(1)}, f32[4,24,128]{2,1,0:T(8,128)S(1)}, f32[3,3,27,64]{3,2,1,0:T(8,128)S(1)}) custom-call(f32[6,6,27,128]{3,2,1,0:T(8,128)S(1)} %bitcast.4, f32[3,3,27,64]{3,2,1,0:T(8,128)S(1)} %bitcast.5, s32[16,32]{1,0:T(8,128)S(1)} %copy-done.2), custom_call_target="tpu_custom_call" | custom-call | tf_op jit(solution)/shard_map/pallas_call | solution.py:112
  23.2 0.0 copy-start.4
  23.2 0.0 copy-done.3
  23.2 0.6 %copy-done.4 = f32[27]{0:T(128)S(1)} copy-done((f32[27]{0:T(128)S(1)}, f32[27]{0:T(128)}, u32[]{:S(2)}) %copy-start.4) | copy-done | bytes 132
  23.9 3.9 %shard_map.69 = (f32[6,6,27,128]{3,2,1,0:T(8,128)}, f32[3,3,27,64]{3,2,1,0:T(8,128)}, f32[27,8,8,128]{3,2,1,0:T(8,128)S(1)}) custom-call(f32[27,8,8,128]{3,2,1,0:T(8,128)S(1)} %get-tuple-element.8.given, f32[4,64,128]{2,1,0:T(8,128)S(1)} %get-tuple-element.9.faces, f32[4,24,128]{2,1,0:T(8,128)S(1)} %get-tuple-element.10.corners, ...), custom_call_target="tpu_custom_call", output_to_operand_aliasing={{2}: (0, {})} | custom-call | tf_op jit(solution)/shard_map/pallas_call | solution.py:403
Async XLA Ops:
  0.6 1.1 %copy-start = (f32[27,6,6,128]{3,0,2,1:T(8,128)S(1)}, f32[27,6,6,128]{3,0,2,1:T(8,128)}, u32[]{:S(2)}) copy-start(f32[27,6,6,128]{3,0,2,1:T(8,128)} %param.5) | copy-start | bytes 1492996
  1.7 0.9 %copy-start.1 = (f32[27,3,3,64]{3,0,2,1:T(8,128)S(1)}, f32[27,3,3,64]{3,0,2,1:T(8,128)}, u32[]{:S(2)}) copy-start(f32[27,3,3,64]{3,0,2,1:T(8,128)} %param.6) | copy-start | bytes 186628
  2.6 0.7 %copy-start.2 = (s32[16,32]{1,0:T(8,128)S(1)}, s32[16,32]{1,0:T(8,128)}, u32[]{:S(2)}) copy-start(s32[16,32]{1,0:T(8,128)} %levels.1) | copy-start | bytes 6148
  3.3 19.9 %copy-start.3 = (s32[6,6,128]{2,1,0:T(8,128)S(1)}, s32[6,6,128]{2,1,0:T(8,128)}, u32[]{:S(2)}) copy-start(s32[6,6,128]{2,1,0:T(8,128)} %obstacle.1) | copy-start | bytes 55300
  23.2 0.7 %copy-start.4 = (f32[27]{0:T(128)S(1)}, f32[27]{0:T(128)}, u32[]{:S(2)}) copy-start(f32[27]{0:T(128)} %rates.1) | copy-start | bytes 328
where the time goes:
time: 28 us; the launch traced here: 27.7 us
  Pallas kernels  23.7 us (85%)
  local copies, waits for them, and re-layouts  3.31 us (12%)
  between operations  0.67 us (2%)
    pallas_call x1, Pallas kernels, exchange(): pl.pallas_call(functools.partial(exchange_kernel, n_stream, n_span), out_...  19.9 us
    pallas_call x1, Pallas kernels, step(): pl.pallas_call(functools.partial(step_kernel, n_stream, n_span), out_shap...  3.86 us
    unnamed x10, local copies, waits for them, and re-layouts  3.31 us

commit v1 on v0

v1 whole, which is shorter than its diff:
```python
import functools

import jax
import jax.numpy as jnp
from jax import lax
from jax.experimental import pallas as pl
from jax.experimental.pallas import tpu as pltpu
from jax.sharding import PartitionSpec as P

MESH = pl.DeviceIdType.MESH
F32 = jnp.float32
FACES = ((-1, 0), (1, 0), (0, -1), (0, 1))
CORNERS = ((-1, -1), (-1, 1), (1, -1), (1, 1))


def face_pops(side):
    dx, dy = side
    return [q for q in range(27) if (q // 9 - 1 == -dx if dx else q // 3 % 3 - 1 == -dy)]


def corner_start(side):
    dx, dy = side
    return 9 * (1 - dx) + 3 * (1 - dy)


def face_cells(side):
    dx, dy = side
    return [(1 - dx, j) for j in range(3)] if dx else [(i, 1 - dy) for i in range(3)]


def end_pops(side):
    dx, dy = side
    return [face_pops((0, s) if dx else (s, 0)) for s in (-1, 1)]


def pick_rows(cell, pops):
    return jnp.concatenate([cell[q : q + 3] for q in pops[::3]], axis=0)


def exchange_kernel(
    n_stream, n_span, fine, coarse, obstacle, level, rates,
    turned, faces, corners, tall, own, flags, table, around,
    native, levels, speeds, face_out, corner_out, load_sem, send_sem, recv_sem,
):
    row, col = lax.axis_index("stream"), lax.axis_index("span")

    def at(side):
        return (lax.rem(row + side[0] + n_stream, n_stream), lax.rem(col + side[1] + n_span, n_span))

    barrier = pltpu.get_barrier_semaphore()
    loads = [
        pltpu.make_async_copy(fine, native, load_sem.at[0]),
        pltpu.make_async_copy(coarse, own, load_sem.at[1]),
        pltpu.make_async_copy(level, levels, load_sem.at[2]),
        pltpu.make_async_copy(obstacle, flags, load_sem.at[3]),
        pltpu.make_async_copy(rates, speeds, load_sem.at[4]),
    ]
    for load in loads:
        load.start()
    for side in CORNERS + FACES:
        pl.semaphore_signal(barrier, inc=1, device_id=at(side), device_id_type=MESH)
    for load in loads[:3]:
        load.wait()
    here = levels[row, col]
    there = [levels[at(side)[0], at(side)[1]] for side in FACES + CORNERS]
    for slot, side in enumerate(CORNERS):
        dx, dy = side
        cell = own[1 - dx, 1 - dy]
        corner_out[slot, pl.ds(0, 14), :] = jnp.concatenate([cell[0:14], cell[13:27]], axis=1)
        corner_out[slot, pl.ds(14, 3), :] = native[
            5 if dx < 0 else 0, 5 if dy < 0 else 0, pl.ds(corner_start(side), 3), :
        ]
    for slot, side in enumerate(FACES):
        dx, dy = side
        both = (here == 1) & (there[FACES.index((-dx, -dy))] == 1)
        cells = [own[i, j] for i, j in face_cells(side)]
        face_out[slot, pl.ds(0, 27), :] = jnp.concatenate([cells[0], cells[1]], axis=1)
        face_out[slot, pl.ds(27, 27), :] = jnp.concatenate([cells[2], cells[2]], axis=1)
        edge = native[5 if dx < 0 else 0] if dx else native[:, 5 if dy < 0 else 0]
        edge = jnp.swapaxes(edge, 0, 1)
        for n, q in enumerate(face_pops(side)):
            spot = face_out.at[slot, pl.ds(6 * n, 6)]
            spot[...] = jnp.where(both, edge[q], spot[...])
        ends = [pick_rows(cell, pops) for cell, pops in zip((cells[0], cells[2]), end_pops(side))]
        face_out[slot, pl.ds(54, 9), :] = jnp.concatenate(ends, axis=1)
    pl.semaphore_wait(barrier, 8)
    copies = []
    for slot, (dx, dy) in enumerate(CORNERS):
        copies.append(
            pltpu.make_async_remote_copy(
                corner_out.at[slot, pl.ds(0, 17)], corners.at[slot, pl.ds(0, 17)],
                send_sem.at[4 + slot], recv_sem.at[4 + slot], device_id=at((-dx, -dy)), device_id_type=MESH,
            )
        )
    for slot, (dx, dy) in enumerate(FACES):
        copies.append(
            pltpu.make_async_remote_copy(
                face_out.at[slot, pl.ds(0, 63)], faces.at[slot, pl.ds(0, 63)],
                send_sem.at[slot], recv_sem.at[slot], device_id=at((-dx, -dy)), device_id_type=MESH,
            )
        )
    for copy in copies:
        copy.start()
    for x in range(6):
        turned[:, x + 1, pl.ds(1, 6), :] = jnp.swapaxes(native[x], 0, 1)
    for i in range(3):
        for j in range(3):
            cell = own[i, j]
            tall[i, j] = stretch(jnp.concatenate([cell, cell], axis=1))
    for n, value in enumerate([here] + there):
        around[n] = jnp.full((8, 128), value, jnp.int32)
    for load in loads[3:]:
        load.wait()
    for q in range(27):
        orders = (q // 9, q // 3 % 3, q % 3)
        share = 0.0 if 1 in orders else 0.125 / 3.0 ** orders.count(2)
        fine_rate = jnp.full((1, 128), speeds[q], F32)
        for n, rate in enumerate((fine_rate, 1.0 / (2.0 / fine_rate - 0.5))):
            table[n, 0, pl.ds(q, 1), :] = (1.0 - rate) * 0.125
            table[n, 1, pl.ds(q, 1), :] = rate * share
    for copy in copies:
        copy.wait()


def exchange(n_stream, n_span, *args):
    hbm = pl.BlockSpec(memory_space=pltpu.HBM)
    vmem = pl.BlockSpec(memory_space=pltpu.VMEM)
    return pl.pallas_call(
        functools.partial(exchange_kernel, n_stream, n_span),
        out_shape=(
            jax.ShapeDtypeStruct((27, 8, 8, 128), F32),
            jax.ShapeDtypeStruct((4, 64, 128), F32),
            jax.ShapeDtypeStruct((4, 24, 128), F32),
            jax.ShapeDtypeStruct((3, 3, 27, 128), F32),
            jax.ShapeDtypeStruct((3, 3, 27, 64), F32),
            jax.ShapeDtypeStruct((6, 6, 128), jnp.int32),
            jax.ShapeDtypeStruct((2, 2, 32, 128), F32),
            jax.ShapeDtypeStruct((9, 8, 128), jnp.int32),
        ),
        in_specs=[hbm] * 5,
        out_specs=(vmem,) * 8,
        scratch_shapes=[
            pltpu.VMEM((6, 6, 27, 128), F32),
            pltpu.SMEM((16, 32), jnp.int32),
            pltpu.SMEM((27,), F32),
            pltpu.VMEM((4, 64, 128), F32),
            pltpu.VMEM((4, 24, 128), F32),
            pltpu.SemaphoreType.DMA((5,)),
            pltpu.SemaphoreType.DMA((8,)),
            pltpu.SemaphoreType.DMA((8,)),
        ],
        compiler_params=pltpu.CompilerParams(
            collective_id=0, has_side_effects=True, vmem_limit_bytes=24 * 2**20
        ),
    )(*args)


def forward(low, mid, high, speed, total=None):
    pair, diff = high + low, high - low
    if total is None:
        total = pair + 4.0 * mid
    first = diff - speed * total
    return total, first, pair - speed * (diff + first)


def backward(total, first, second, speed):
    slope = first + speed * total
    curve = second + speed * (first + slope)
    return curve - slope, 0.5 * (total - curve), curve + slope


def collide(g, keep, pull):
    t0 = [g[r] + g[18 + r] + 4.0 * g[9 + r] for r in range(9)]
    dx = [g[18 + r] - g[r] for r in range(9)]
    s0 = [t0[c] + t0[6 + c] + 4.0 * t0[3 + c] for c in range(3)]
    dy = [t0[6 + c] - t0[c] for c in range(3)]
    density = s0[0] + s0[2] + 4.0 * s0[1]
    ex = [dx[c] + dx[6 + c] + 4.0 * dx[3 + c] for c in range(3)]
    inverse = 1.0 / density
    ux = (ex[0] + ex[2] + 4.0 * ex[1]) * inverse
    uy = (dy[0] + dy[2] + 4.0 * dy[1]) * inverse
    uz = (s0[2] - s0[0]) * inverse
    k = [None] * 27
    for r in range(9):
        k[r], k[9 + r], k[18 + r] = forward(g[r], g[9 + r], g[18 + r], ux, t0[r])
    for a in range(3):
        for c in range(3):
            i = 9 * a + c
            k[i], k[i + 3], k[i + 6] = forward(k[i], k[i + 3], k[i + 6], uy, s0[c] if a == 0 else None)
    for i in range(0, 27, 3):
        k[i], k[i + 1], k[i + 2] = forward(k[i], k[i + 1], k[i + 2], uz, density if i == 0 else None)
    for q in range(27):
        k[q] = keep[q] * k[q] if 1 in (q // 9, q // 3 % 3, q % 3) else keep[q] * k[q] + pull[q] * density
    for i in range(0, 27, 3):
        k[i], k[i + 1], k[i + 2] = backward(k[i], k[i + 1], k[i + 2], uz)
    for a in range(3):
        for c in range(3):
            i = 9 * a + c
            k[i], k[i + 3], k[i + 6] = backward(k[i], k[i + 3], k[i + 6], uy)
    for r in range(9):
        k[r], k[9 + r], k[18 + r] = backward(k[r], k[9 + r], k[18 + r], ux)
    return k


def lane(shape):
    return lax.broadcasted_iota(jnp.int32, shape, len(shape) - 1)


def take(values, index):
    return jnp.take_along_axis(values, index, axis=1)


def stretch(values):
    at = lane(values.shape)
    middle = lax.shift_right_logical(at, 1)
    beside = jnp.clip(middle + 2 * (at & 1) - 1, 0, 63)
    return 0.75 * take(values, middle) + 0.25 * take(values, beside)


def shrink(values):
    at = lane(values.shape)
    even = jnp.minimum(2 * at, 126)
    return (take(values, even) + take(values, even + 1)) * 0.125


def mix(near, far):
    return 0.75 * near + 0.25 * far


def step_kernel(
    given, faces, corners, own_tall, own, obstacle, table, around, fine_next, coarse_next, turned,
    halo, tall, blocked, rolled, coarse_blocked, fine_out, coarse_out, fine_sem, coarse_sem,
):
    def level(n, rows):
        return around[n, pl.ds(0, rows), :] == 1

    def fine_copy(i):
        return pltpu.make_async_copy(fine_out.at[pl.ds(2 * i, 2)], fine_next.at[pl.ds(2 * i, 2)], fine_sem.at[i])

    def coarse_copy():
        return pltpu.make_async_copy(coarse_out, coarse_next, coarse_sem)

    def rates(n):
        return [table[n, 0, pl.ds(q, 1), :] for q in range(27)], [table[n, 1, pl.ds(q, 1), :] for q in range(27)]

    refined = jnp.max(around[0]) == 1

    def halo_cells(side):
        dx, dy = side
        return [(2 + 2 * dx, 1 + j) if dx else (1 + j, 2 + 2 * dy) for j in range(3)]

    def received(raw):
        for slot, (dx, dy) in enumerate(CORNERS):
            both = corners[slot, pl.ds(0, 14), :]
            other = pltpu.roll(both, 64, 1)
            if raw:
                halo[2 + 2 * dx, 2 + 2 * dy, pl.ds(13, 14), :] = other
                halo[2 + 2 * dx, 2 + 2 * dy, pl.ds(0, 14), :] = both
            tall[2 + 2 * dx, 2 + 2 * dy, pl.ds(13, 14), :] = stretch(other)
            tall[2 + 2 * dx, 2 + 2 * dy, pl.ds(0, 14), :] = stretch(both)
        for slot, side in enumerate(FACES):
            spots = halo_cells(side)
            pair = faces[slot, pl.ds(0, 27), :]
            for spot, cell in zip(spots, (pair, pltpu.roll(pair, 64, 1), faces[slot, pl.ds(27, 27), :])):
                if raw:
                    halo[spot[0], spot[1], pl.ds(0, 27), :] = cell
                tall[spot[0], spot[1], pl.ds(0, 27), :] = stretch(cell)
        for i in range(3):
            for j in range(3):
                if raw:
                    halo[i + 1, j + 1, pl.ds(0, 27), pl.ds(0, 64)] = own[i, j]

    def tall_at(i, j, start, count):
        if 0 < i < 4 and 0 < j < 4:
            return own_tall[i - 1, j - 1, pl.ds(start, count), :]
        return tall[i, j, pl.ds(start, count), :]

    @pl.when(refined)
    def _():
        received(False)
        for slot, side in enumerate(FACES):
            ends = faces[slot, pl.ds(54, 9), :]
            spots = halo_cells(side)
            take_ends = level(1 + slot, 1)
            for spot, pops, rows in zip((spots[0], spots[2]), end_pops(side), (ends, pltpu.roll(ends, 64, 1))):
                rows = stretch(rows)
                for n in (0, 3, 6):
                    place = tall.at[spot[0], spot[1], pl.ds(pops[n], 3)]
                    place[...] = jnp.where(take_ends, rows[n : n + 3], place[...])
        for slot, side in enumerate(FACES):
            dx, dy = side
            pops = face_pops(side)
            edge, inner = 2 + 2 * (dx + dy), 2 + (dx + dy)
            rim = 7 if dx + dy > 0 else 0
            first, count = (pops[0], 9) if dx else (0, 27)
            if dx:
                line = [mix(tall_at(edge, j, first, count), tall_at(inner, j, first, count)) for j in range(5)]
            else:
                line = [mix(tall_at(i, edge, first, count), tall_at(i, inner, first, count)) for i in range(5)]
            cells = []
            for n in range(6):
                cells.append(mix(line[n // 2 + 1], line[n // 2 + 2 * (n % 2)]))
            turn = jnp.swapaxes(jnp.stack(cells), 0, 1)
            fine_there = level(1 + slot, 6)
            for n, q in enumerate(pops):
                values = jnp.where(fine_there, faces[slot, pl.ds(6 * n, 6), :], turn[q - first])
                if dx:
                    turned[q, rim, pl.ds(1, 6), :] = values
                else:
                    turned[q, pl.ds(1, 6), rim, :] = values

        for slot, side in enumerate(CORNERS):
            dx, dy = side
            start = corner_start(side)
            ei, ii, ej, ij = 2 + 2 * dx, 2 + dx, 2 + 2 * dy, 2 + dy
            exploded = mix(
                mix(tall_at(ei, ej, start, 3), tall_at(ii, ej, start, 3)),
                mix(tall_at(ei, ij, start, 3), tall_at(ii, ij, start, 3)),
            )
            value = jnp.where(level(5 + slot, 3), corners[slot, pl.ds(14, 3), :], exploded)
            for c in range(3):
                turned[start + c, 7 if dx > 0 else 0, pl.ds(7 if dy > 0 else 0, 1), :] = value[c : c + 1]

        blocked[...] = jnp.zeros_like(blocked)
        blocked[pl.ds(1, 6), pl.ds(1, 6), :] = obstacle[...]
        at = lane((8, 128))
        for x in range(8):
            flags = blocked[x]
            rolled[1, x] = flags
            rolled[2, x] = jnp.where(at == 0, 1, pltpu.roll(flags, 1, 1))
            rolled[0, x] = jnp.where(at == 127, 1, pltpu.roll(flags, 127, 1))

        def line(x):
            keep, pull = rates(0)
            g = []
            for q in range(27):
                ex, ey, ez = q // 9 - 1, q // 3 % 3 - 1, q % 3 - 1
                source = turned[q, x + 1 - ex, pl.ds(1 - ey, 6), :]
                if ez:
                    source = pltpu.roll(source, ez % 128, 1)
                if q == 13:
                    g.append(source)
                    continue
                stop = rolled[ez + 1, x + 1 - ex, pl.ds(1 - ey, 6), :]
                g.append(jnp.where(stop != 0, turned[26 - q, x + 1, pl.ds(1, 6), :], source))
            new = collide(g, keep, pull)
            wall = blocked[x + 1, pl.ds(1, 6), :] != 0
            new = [jnp.where(wall, turned[q, x + 1, pl.ds(1, 6), :], new[q]) for q in range(27)]
            fine_out[x] = jnp.swapaxes(jnp.stack(new), 0, 1)

        def lines(i, carry):
            line(2 * i)
            line(2 * i + 1)
            fine_copy(i).start()
            for j in range(3):
                total = (fine_out[2 * i, 2 * j] + fine_out[2 * i, 2 * j + 1]) + (
                    fine_out[2 * i + 1, 2 * j] + fine_out[2 * i + 1, 2 * j + 1]
                )
                coarse_out[i, j] = shrink(total)[:, :64]
            return carry

        lax.fori_loop(0, 3, lines, 0)
        coarse_copy().start()

    @pl.when(jnp.logical_not(refined))
    def _():
        received(True)
        for i in range(3):
            for x in (2 * i, 2 * i + 1):
                line = [mix(tall_at(i + 1, j, 0, 27), tall_at(i + 2 * (x % 2), j, 0, 27)) for j in range(5)]
                for y in range(6):
                    fine_out[x, y] = mix(line[y // 2 + 1], line[y // 2 + 2 * (y % 2)])
            fine_copy(i).start()

        keep, pull = rates(1)
        flat = turned.reshape(27 * 64, 128)
        for i in range(5):
            cells = jnp.swapaxes(halo[i, :, pl.ds(0, 27), :], 0, 1)
            for q in range(27):
                flat[pl.ds(64 * q + 5 * i, 5), :] = cells[q]
        column = jnp.maximum(
            jnp.maximum(obstacle[2, pl.ds(2, 1), :], obstacle[2, pl.ds(3, 1), :]),
            jnp.maximum(obstacle[3, pl.ds(2, 1), :], obstacle[3, pl.ds(3, 1), :]),
        )
        wide = jnp.broadcast_to(column, (8, 128))
        at = lane((8, 128))
        even = jnp.minimum(2 * at, 126)
        flags = jnp.maximum(take(wide, even), take(wide, even + 1))
        flags = jnp.where(at < 64, flags, 0)
        coarse_blocked[...] = jnp.zeros_like(coarse_blocked)
        coarse_blocked[1, pl.ds(12, 1), :] = flags[:1]
        high = lane((32, 128))
        coarse_blocked[2] = jnp.where(high == 0, 1, pltpu.roll(coarse_blocked[1], 1, 1))
        coarse_blocked[0] = jnp.where(high == 63, 1, pltpu.roll(coarse_blocked[1], 127, 1))
        g = []
        for q in range(27):
            ex, ey, ez = q // 9 - 1, q // 3 % 3 - 1, q % 3 - 1
            start = 6 - 5 * ex - ey
            source = flat[pl.ds(64 * q + start, 13), :]
            if ez:
                source = pltpu.roll(source, ez % 128, 1)
            if q != 13:
                stop = coarse_blocked[ez + 1, pl.ds(start, 13), :]
                source = jnp.where(stop != 0, flat[pl.ds(64 * (26 - q) + 6, 13), :], source)
            g.append(source)
        new = collide(g, keep, pull)
        wall = coarse_blocked[1, pl.ds(6, 13), :] != 0
        new = [jnp.where(wall, flat[pl.ds(64 * q + 6, 13), :], new[q]) for q in range(27)]
        turn = jnp.swapaxes(jnp.stack(new), 0, 1)
        for i in range(3):
            for j in range(3):
                coarse_out[i, j] = turn[5 * i + j][:, :64]
        coarse_copy().start()

    for i in range(3):
        fine_copy(i).wait()
    coarse_copy().wait()


def step(*args):
    vmem = pl.BlockSpec(memory_space=pltpu.VMEM)
    hbm = pl.BlockSpec(memory_space=pltpu.HBM)
    return pl.pallas_call(
        step_kernel,
        out_shape=(
            jax.ShapeDtypeStruct((6, 6, 27, 128), F32),
            jax.ShapeDtypeStruct((3, 3, 27, 64), F32),
            jax.ShapeDtypeStruct((27, 8, 8, 128), F32),
        ),
        in_specs=[vmem] * 8,
        out_specs=(hbm, hbm, vmem),
        input_output_aliases={0: 2},
        scratch_shapes=[
            pltpu.VMEM((5, 5, 32, 128), F32),
            pltpu.VMEM((5, 5, 32, 128), F32),
            pltpu.VMEM((8, 8, 128), jnp.int32),
            pltpu.VMEM((3, 8, 8, 128), jnp.int32),
            pltpu.VMEM((3, 32, 128), jnp.int32),
            pltpu.VMEM((6, 6, 27, 128), F32),
            pltpu.VMEM((3, 3, 27, 64), F32),
            pltpu.SemaphoreType.DMA((3,)),
            pltpu.SemaphoreType.DMA,
        ],
        compiler_params=pltpu.CompilerParams(vmem_limit_bytes=24 * 2**20),
    )(*args)


def solution(mesh):
    n_stream, n_span = mesh.shape["stream"], mesh.shape["span"]

    def local(fine_pops, coarse_pops, obstacle, block_level, relax_rates):
        fine = jnp.transpose(fine_pops, (1, 2, 0, 3))
        coarse = jnp.transpose(coarse_pops, (1, 2, 0, 3))
        ready = exchange(n_stream, n_span, fine, coarse, obstacle, block_level, relax_rates)
        fine_next, coarse_next, _ = step(*ready)
        return jnp.transpose(fine_next, (2, 0, 1, 3)), jnp.transpose(coarse_next, (2, 0, 1, 3))

    placed = P(None, "stream", "span", None)
    return jax.shard_map(
        local,
        mesh=mesh,
        in_specs=(placed, placed, P("stream", "span", None), P(), P()),
        out_specs=(placed, placed),
        check_vma=False,
    )
```

time: 28 us -> 27.2 us (0.971)
  Pallas kernels: 23.7 us -> 22.2 us
  local copies, waits for them, and re-layouts: 3.31 us -> 4.05 us
    pallas_call x1, Pallas kernels: 3.86 us -> 2.89 us  [step(): pl.pallas_call(step_kernel, out_shape=(jax.ShapeDtypeStruct((6, 6, 27, 12...]
    unnamed x10, local copies, waits for them, and re-layouts: 3.31 us -> 4.05 us
    pallas_call x1, Pallas kernels: 19.9 us -> 19.3 us  [exchange(): pl.pallas_call(functools.partial(exchange_kernel, n_stream, n_span), out_...]
where the time goes in v1:
time: 27.2 us; the launch traced here: 26.9 us
  Pallas kernels  22.2 us (82%)
  local copies, waits for them, and re-layouts  4.05 us (15%)
  between operations  0.65 us (2%)
    pallas_call x1, Pallas kernels, exchange(): pl.pallas_call(functools.partial(exchange_kernel, n_stream, n_span), out_...  19.3 us
    unnamed x10, local copies, waits for them, and re-layouts  4.05 us
    pallas_call x1, Pallas kernels, step(): pl.pallas_call(step_kernel, out_shape=(jax.ShapeDtypeStruct((6, 6, 27, 12...  2.89 us

profile of v1, /device:TPU:1, one launch (start us, length us, event | category | flops | bytes accessed | tf_op | source)
XLA Modules:
  0.0 26.9 jit_solution(15959370583742515639)
XLA Ops:
  0.6 0.0 copy-start.4
  0.6 0.6 %copy-done.4 = f32[27]{0:T(128)S(1)} copy-done((f32[27]{0:T(128)S(1)}, f32[27]{0:T(128)}, u32[]{:S(2)}) %copy-start.4) | copy-done | bytes 132
  1.3 0.0 copy-start
  1.3 1.1 %copy-done = f32[27,6,6,128]{3,0,2,1:T(8,128)S(1)} copy-done((f32[27,6,6,128]{3,0,2,1:T(8,128)S(1)}, f32[27,6,6,128]{3,0,2,1:T(8,128)}, u32[]{:S(2)}) %copy-start) | copy-done | bytes 497688
  2.4 0.0 copy-start.1
  2.4 0.9 %copy-done.1 = f32[27,3,3,64]{3,0,2,1:T(8,128)S(1)} copy-done((f32[27,3,3,64]{3,0,2,1:T(8,128)S(1)}, f32[27,3,3,64]{3,0,2,1:T(8,128)}, u32[]{:S(2)}) %copy-start.1) | copy-done | bytes 62232
  3.3 0.0 copy-start.2
  3.3 0.7 %copy-done.2 = s32[6,6,128]{2,1,0:T(8,128)S(1)} copy-done((s32[6,6,128]{2,1,0:T(8,128)S(1)}, s32[6,6,128]{2,1,0:T(8,128)}, u32[]{:S(2)}) %copy-start.2) | copy-done | bytes 18456
  4.0 0.0 copy-start.3
  4.0 0.7 %copy-done.3 = s32[16,32]{1,0:T(8,128)S(1)} copy-done((s32[16,32]{1,0:T(8,128)S(1)}, s32[16,32]{1,0:T(8,128)}, u32[]{:S(2)}) %copy-start.3) | copy-done | bytes 2072
  4.7 19.3 %shard_map.68 = (f32[27,8,8,128]{3,2,1,0:T(8,128)S(1)}, f32[4,64,128]{2,1,0:T(8,128)S(1)}, f32[4,24,128]{2,1,0:T(8,128)S(1)}, f32[3,3,27,128]{3,2,1,0:T(8,128)S(...) custom-call(f32[6,6,27,128]{3,2,1,0:T(8,128)S(1)} %bitcast.4, ...), custom_call_target="tpu_custom_call" | custom-call | tf_op jit(solution)/shard_map/pallas_call | solution.py:128
  24.0 2.9 %shard_map.69 = (f32[6,6,27,128]{3,2,1,0:T(8,128)}, f32[3,3,27,64]{3,2,1,0:T(8,128)}, f32[27,8,8,128]{3,2,1,0:T(8,128)S(1)}) custom-call(f32[27,8,8,128]{3,2,1,0:T(8,128)S(1)} %get-tuple-element.12.given, f32[4,64,128]{2,1,0:T(8,128)S(1)} %get-tuple-element.13.faces, f32[4,24,128]{2,1,0:T(8,128)S(1)} %get-tuple-element.14.corners, ...), custom_call_target="tpu_custom_call", output_to_operand_aliasing={{2}: (0, {})} | custom-call | tf_op jit(solution)/shard_map/pallas_call | solution.py:423
Async XLA Ops:
  0.6 0.7 %copy-start.4 = (f32[27]{0:T(128)S(1)}, f32[27]{0:T(128)}, u32[]{:S(2)}) copy-start(f32[27]{0:T(128)} %rates.1) | copy-start | bytes 328
  1.3 1.1 %copy-start = (f32[27,6,6,128]{3,0,2,1:T(8,128)S(1)}, f32[27,6,6,128]{3,0,2,1:T(8,128)}, u32[]{:S(2)}) copy-start(f32[27,6,6,128]{3,0,2,1:T(8,128)} %param.5) | copy-start | bytes 1492996
  2.4 0.9 %copy-start.1 = (f32[27,3,3,64]{3,0,2,1:T(8,128)S(1)}, f32[27,3,3,64]{3,0,2,1:T(8,128)}, u32[]{:S(2)}) copy-start(f32[27,3,3,64]{3,0,2,1:T(8,128)} %param.6) | copy-start | bytes 186628
  3.3 0.7 %copy-start.2 = (s32[6,6,128]{2,1,0:T(8,128)S(1)}, s32[6,6,128]{2,1,0:T(8,128)}, u32[]{:S(2)}) copy-start(s32[6,6,128]{2,1,0:T(8,128)} %obstacle.1) | copy-start | bytes 55300
  4.0 0.7 %copy-start.3 = (s32[16,32]{1,0:T(8,128)S(1)}, s32[16,32]{1,0:T(8,128)}, u32[]{:S(2)}) copy-start(s32[16,32]{1,0:T(8,128)} %level.1) | copy-start | bytes 6148

commit v2 on v1

--- a/solution.py
+++ b/solution.py
@@ -152,7 +152,7 @@
         compiler_params=pltpu.CompilerParams(
             collective_id=0, has_side_effects=True, vmem_limit_bytes=24 * 2**20
         ),
-    )(*args)
+    )(*[pltpu.with_memory_space_constraint(arg, pltpu.HBM) for arg in args])
 
 
 def forward(low, mid, high, speed, total=None):

time: 27.2 us -> 22.9 us (0.84)
  local copies, waits for them, and re-layouts: 4.05 us -> 0 us
    unnamed x10 -> x0, local copies, waits for them, and re-layouts: 4.05 us -> none
where the time goes in v2:
time: 22.9 us; the launch traced here: 22.8 us
  Pallas kernels  22.2 us (97%)
  between operations  0.64 us (3%)
    pallas_call x1, Pallas kernels, exchange(): pl.pallas_call(functools.partial(exchange_kernel, n_stream, n_span), out_...  19.3 us
    pallas_call x1, Pallas kernels, step(): pl.pallas_call(step_kernel, out_shape=(jax.ShapeDtypeStruct((6, 6, 27, 12...  2.88 us

profile of v2, /device:TPU:1, one launch (start us, length us, event | category | flops | bytes accessed | tf_op | source)
XLA Modules:
  0.0 22.8 jit_solution(10281136121479339190)
XLA Ops:
  0.6 19.3 %shard_map.68 = (f32[27,8,8,128]{3,2,1,0:T(8,128)S(1)}, f32[4,64,128]{2,1,0:T(8,128)S(1)}, f32[4,24,128]{2,1,0:T(8,128)S(1)}, f32[3,3,27,128]{3,2,1,0:T(8,128)S(...) custom-call(f32[6,6,27,128]{3,2,1,0:T(8,128)} %bitcast.4, ...), custom_call_target="tpu_custom_call" | custom-call | tf_op jit(solution)/shard_map/pallas_call | solution.py:128
  19.9 2.9 %shard_map.69 = (f32[6,6,27,128]{3,2,1,0:T(8,128)}, f32[3,3,27,64]{3,2,1,0:T(8,128)}, f32[27,8,8,128]{3,2,1,0:T(8,128)S(1)}) custom-call(f32[27,8,8,128]{3,2,1,0:T(8,128)S(1)} %get-tuple-element.12.given, f32[4,64,128]{2,1,0:T(8,128)S(1)} %get-tuple-element.13.faces, f32[4,24,128]{2,1,0:T(8,128)S(1)} %get-tuple-element.14.corners, ...), custom_call_target="tpu_custom_call", output_to_operand_aliasing={{2}: (0, {})} | custom-call | tf_op jit(solution)/shard_map/pallas_call | solution.py:423

commit v3 on v2

--- a/solution.py
+++ b/solution.py
@@ -37,10 +37,14 @@
     return jnp.concatenate([cell[q : q + 3] for q in pops[::3]], axis=0)
 
 
+def rates_of(table, n):
+    return [table[n, 0, pl.ds(q, 1), :] for q in range(27)], [table[n, 1, pl.ds(q, 1), :] for q in range(27)]
+
+
 def exchange_kernel(
     n_stream, n_span, fine, coarse, obstacle, level, rates,
-    turned, faces, corners, tall, own, flags, table, around,
-    native, levels, speeds, face_out, corner_out, load_sem, send_sem, recv_sem,
+    turned, faces, corners, tall, own, inner, coarse_stop, table, around,
+    native, flags, levels, speeds, blocked, rolled, face_out, corner_out, load_sem, send_sem, recv_sem,
 ):
     row, col = lax.axis_index("stream"), lax.axis_index("span")
 
@@ -118,6 +122,47 @@
         for n, rate in enumerate((fine_rate, 1.0 / (2.0 / fine_rate - 0.5))):
             table[n, 0, pl.ds(q, 1), :] = (1.0 - rate) * 0.125
             table[n, 1, pl.ds(q, 1), :] = rate * share
+    blocked[...] = jnp.zeros_like(blocked)
+    blocked[pl.ds(1, 6), pl.ds(1, 6), :] = flags[...]
+    rows = lane((8, 128))
+    for x in range(8):
+        stop = blocked[x]
+        rolled[1, x] = stop
+        rolled[2, x] = jnp.where(rows == 0, 1, pltpu.roll(stop, 1, 1))
+        rolled[0, x] = jnp.where(rows == 127, 1, pltpu.roll(stop, 127, 1))
+    stop = jnp.maximum(jnp.maximum(blocked[3], blocked[4]), pltpu.roll(jnp.maximum(blocked[3], blocked[4]), 7, 0))
+    even = jnp.minimum(2 * rows, 126)
+    stop = jnp.where(rows < 64, jnp.maximum(take(stop, even), take(stop, even + 1)), 0)
+    coarse_stop[...] = jnp.zeros_like(coarse_stop)
+    coarse_stop[1, pl.ds(12, 1), :] = stop[3:4]
+    high = lane((32, 128))
+    coarse_stop[2] = jnp.where(high == 0, 1, pltpu.roll(coarse_stop[1], 1, 1))
+    coarse_stop[0] = jnp.where(high == 63, 1, pltpu.roll(coarse_stop[1], 127, 1))
+
+    def middle(x, carry):
+        keep, pull = rates_of(table, 0)
+        g = []
+        for q in range(27):
+            ex, ey, ez = q // 9 - 1, q // 3 % 3 - 1, q % 3 - 1
+            source = turned[q, x + 1 - ex, pl.ds(1 - ey, 6), :]
+            if ez:
+                source = pltpu.roll(source, ez % 128, 1)
+            if q != 13:
+                stop = rolled[ez + 1, x + 1 - ex, pl.ds(1 - ey, 6), :]
+                source = jnp.where(stop != 0, turned[26 - q, x + 1, pl.ds(1, 6), :], source)
+            g.append(source)
+        new = collide(g, keep, pull)
+        wall = blocked[x + 1, pl.ds(1, 6), :] != 0
+        new = [jnp.where(wall, turned[q, x + 1, pl.ds(1, 6), :], new[q]) for q in range(27)]
+        inner[x - 1] = jnp.swapaxes(jnp.stack(new), 0, 1)[1:5]
+        return carry
+
+    lax.fori_loop(1, 5, middle, 0)
+    for x in range(1, 5):
+        line = [mix(tall[x // 2, j], tall[x // 2 - 1 + 2 * (x % 2), j]) for j in range(3)]
+        for y in range(1, 5):
+            exploded = mix(line[y // 2], line[y // 2 - 1 + 2 * (y % 2)])
+            inner[x - 1, y - 1] = jnp.where(here == 1, inner[x - 1, y - 1], exploded)
     for copy in copies:
         copy.wait()
 
@@ -133,16 +178,20 @@
             jax.ShapeDtypeStruct((4, 24, 128), F32),
             jax.ShapeDtypeStruct((3, 3, 27, 128), F32),
             jax.ShapeDtypeStruct((3, 3, 27, 64), F32),
-            jax.ShapeDtypeStruct((6, 6, 128), jnp.int32),
+            jax.ShapeDtypeStruct((4, 4, 27, 128), F32),
+            jax.ShapeDtypeStruct((3, 32, 128), jnp.int32),
             jax.ShapeDtypeStruct((2, 2, 32, 128), F32),
             jax.ShapeDtypeStruct((9, 8, 128), jnp.int32),
         ),
         in_specs=[hbm] * 5,
-        out_specs=(vmem,) * 8,
+        out_specs=(vmem,) * 9,
         scratch_shapes=[
             pltpu.VMEM((6, 6, 27, 128), F32),
+            pltpu.VMEM((6, 6, 128), jnp.int32),
             pltpu.SMEM((16, 32), jnp.int32),
             pltpu.SMEM((27,), F32),
+            pltpu.VMEM((8, 8, 128), jnp.int32),
+            pltpu.VMEM((3, 8, 8, 128), jnp.int32),
             pltpu.VMEM((4, 64, 128), F32),
             pltpu.VMEM((4, 24, 128), F32),
             pltpu.SemaphoreType.DMA((5,)),
@@ -228,20 +277,26 @@
 
 
 def step_kernel(
-    given, faces, corners, own_tall, own, obstacle, table, around, fine_next, coarse_next, turned,
-    halo, tall, blocked, rolled, coarse_blocked, fine_out, coarse_out, fine_sem, coarse_sem,
+    given, faces, corners, own_tall, own, inner, coarse_stop, table, around, fine_next, coarse_next, turned,
+    halo, tall, edge_x, edge_y, coarse_out, sems,
 ):
+    inner_copy = pltpu.make_async_copy(inner, fine_next.at[pl.ds(1, 4), pl.ds(1, 4)], sems.at[0])
+    inner_copy.start()
+    x_copies = [pltpu.make_async_copy(edge_x.at[n], fine_next.at[5 * n], sems.at[1 + n]) for n in range(2)]
+    y_copies = [
+        pltpu.make_async_copy(edge_y.at[n], fine_next.at[pl.ds(1, 4), 5 * n], sems.at[3 + n]) for n in range(2)
+    ]
+    coarse_copy = pltpu.make_async_copy(coarse_out, coarse_next, sems.at[5])
+
     def level(n, rows):
         return around[n, pl.ds(0, rows), :] == 1
 
-    def fine_copy(i):
-        return pltpu.make_async_copy(fine_out.at[pl.ds(2 * i, 2)], fine_next.at[pl.ds(2 * i, 2)], fine_sem.at[i])
-
-    def coarse_copy():
-        return pltpu.make_async_copy(coarse_out, coarse_next, coarse_sem)
-
-    def rates(n):
-        return [table[n, 0, pl.ds(q, 1), :] for q in range(27)], [table[n, 1, pl.ds(q, 1), :] for q in range(27)]
+    def cell(x, y):
+        if x % 5 == 0:
+            return edge_x[x // 5, y]
+        if y % 5 == 0:
+            return edge_y[y // 5, x - 1]
+        return inner[x - 1, y - 1]
 
     refined = jnp.max(around[0]) == 1
 
@@ -321,77 +376,62 @@
             for c in range(3):
                 turned[start + c, 7 if dx > 0 else 0, pl.ds(7 if dy > 0 else 0, 1), :] = value[c : c + 1]
 
-        blocked[...] = jnp.zeros_like(blocked)
-        blocked[pl.ds(1, 6), pl.ds(1, 6), :] = obstacle[...]
-        at = lane((8, 128))
-        for x in range(8):
-            flags = blocked[x]
-            rolled[1, x] = flags
-            rolled[2, x] = jnp.where(at == 0, 1, pltpu.roll(flags, 1, 1))
-            rolled[0, x] = jnp.where(at == 127, 1, pltpu.roll(flags, 127, 1))
-
-        def line(x):
-            keep, pull = rates(0)
+        keep, pull = rates_of(table, 0)
+
+        def advance(load, count):
+            at = lane((count, 128))
+            still = [load(q, 0, 0) for q in range(27)]
             g = []
             for q in range(27):
                 ex, ey, ez = q // 9 - 1, q // 3 % 3 - 1, q % 3 - 1
-                source = turned[q, x + 1 - ex, pl.ds(1 - ey, 6), :]
+                source = load(q, ex, ey) if ex or ey else still[q]
                 if ez:
-                    source = pltpu.roll(source, ez % 128, 1)
-                if q == 13:
-                    g.append(source)
-                    continue
-                stop = rolled[ez + 1, x + 1 - ex, pl.ds(1 - ey, 6), :]
-                g.append(jnp.where(stop != 0, turned[26 - q, x + 1, pl.ds(1, 6), :], source))
-            new = collide(g, keep, pull)
-            wall = blocked[x + 1, pl.ds(1, 6), :] != 0
-            new = [jnp.where(wall, turned[q, x + 1, pl.ds(1, 6), :], new[q]) for q in range(27)]
-            fine_out[x] = jnp.swapaxes(jnp.stack(new), 0, 1)
-
-        def lines(i, carry):
-            line(2 * i)
-            line(2 * i + 1)
-            fine_copy(i).start()
+                    source = jnp.where(at == (0 if ez > 0 else 127), still[26 - q], pltpu.roll(source, ez % 128, 1))
+                g.append(source)
+            return jnp.swapaxes(jnp.stack(collide(g, keep, pull)), 0, 1)
+
+        for n in range(2):
+            edge_x[n] = advance(lambda q, ex, ey: turned[q, 5 * n + 1 - ex, pl.ds(1 - ey, 6), :], 6)
+            x_copies[n].start()
+        both = advance(
+            lambda q, ex, ey: jnp.concatenate(
+                [turned[q, pl.ds(2 - ex, 4), 1 - ey, :], turned[q, pl.ds(2 - ex, 4), 6 - ey, :]], axis=0
+            ),
+            8,
+        )
+        for n in range(2):
+            edge_y[n] = both[4 * n : 4 * n + 4]
+            y_copies[n].start()
+        for i in range(3):
             for j in range(3):
-                total = (fine_out[2 * i, 2 * j] + fine_out[2 * i, 2 * j + 1]) + (
-                    fine_out[2 * i + 1, 2 * j] + fine_out[2 * i + 1, 2 * j + 1]
+                total = (cell(2 * i, 2 * j) + cell(2 * i, 2 * j + 1)) + (
+                    cell(2 * i + 1, 2 * j) + cell(2 * i + 1, 2 * j + 1)
                 )
                 coarse_out[i, j] = shrink(total)[:, :64]
-            return carry
-
-        lax.fori_loop(0, 3, lines, 0)
-        coarse_copy().start()
+        coarse_copy.start()
 
     @pl.when(jnp.logical_not(refined))
     def _():
         received(True)
-        for i in range(3):
-            for x in (2 * i, 2 * i + 1):
-                line = [mix(tall_at(i + 1, j, 0, 27), tall_at(i + 2 * (x % 2), j, 0, 27)) for j in range(5)]
-                for y in range(6):
-                    fine_out[x, y] = mix(line[y // 2 + 1], line[y // 2 + 2 * (y % 2)])
-            fine_copy(i).start()
-
-        keep, pull = rates(1)
+        for x in range(6):
+            line = [mix(tall_at(x // 2 + 1, j, 0, 27), tall_at(x // 2 + 2 * (x % 2), j, 0, 27)) for j in range(5)]
+            for y in range(6) if x % 5 == 0 else (0, 5):
+                exploded = mix(line[y // 2 + 1], line[y // 2 + 2 * (y % 2)])
+                if x % 5 == 0:
+                    edge_x[x // 5, y] = exploded
+                else:
+                    edge_y[y // 5, x - 1] = exploded
+            if x % 5 == 0:
+                x_copies[x // 5].start()
+        for n in range(2):
+            y_copies[n].start()
+
+        keep, pull = rates_of(table, 1)
         flat = turned.reshape(27 * 64, 128)
         for i in range(5):
             cells = jnp.swapaxes(halo[i, :, pl.ds(0, 27), :], 0, 1)
             for q in range(27):
                 flat[pl.ds(64 * q + 5 * i, 5), :] = cells[q]
-        column = jnp.maximum(
-            jnp.maximum(obstacle[2, pl.ds(2, 1), :], obstacle[2, pl.ds(3, 1), :]),
-            jnp.maximum(obstacle[3, pl.ds(2, 1), :], obstacle[3, pl.ds(3, 1), :]),
-        )
-        wide = jnp.broadcast_to(column, (8, 128))
-        at = lane((8, 128))
-        even = jnp.minimum(2 * at, 126)
-        flags = jnp.maximum(take(wide, even), take(wide, even + 1))
-        flags = jnp.where(at < 64, flags, 0)
-        coarse_blocked[...] = jnp.zeros_like(coarse_blocked)
-        coarse_blocked[1, pl.ds(12, 1), :] = flags[:1]
-        high = lane((32, 128))
-        coarse_blocked[2] = jnp.where(high == 0, 1, pltpu.roll(coarse_blocked[1], 1, 1))
-        coarse_blocked[0] = jnp.where(high == 63, 1, pltpu.roll(coarse_blocked[1], 127, 1))
         g = []
         for q in range(27):
             ex, ey, ez = q // 9 - 1, q // 3 % 3 - 1, q % 3 - 1
@@ -400,21 +440,20 @@
             if ez:
                 source = pltpu.roll(source, ez % 128, 1)
             if q != 13:
-                stop = coarse_blocked[ez + 1, pl.ds(start, 13), :]
+                stop = coarse_stop[ez + 1, pl.ds(start, 13), :]
                 source = jnp.where(stop != 0, flat[pl.ds(64 * (26 - q) + 6, 13), :], source)
             g.append(source)
         new = collide(g, keep, pull)
-        wall = coarse_blocked[1, pl.ds(6, 13), :] != 0
+        wall = coarse_stop[1, pl.ds(6, 13), :] != 0
         new = [jnp.where(wall, flat[pl.ds(64 * q + 6, 13), :], new[q]) for q in range(27)]
         turn = jnp.swapaxes(jnp.stack(new), 0, 1)
         for i in range(3):
             for j in range(3):
                 coarse_out[i, j] = turn[5 * i + j][:, :64]
-        coarse_copy().start()
-
-    for i in range(3):
-        fine_copy(i).wait()
-    coarse_copy().wait()
+        coarse_copy.start()
+
+    for copy in [inner_copy, coarse_copy] + x_copies + y_copies:
+        copy.wait()
 
 
 def step(*args):
@@ -427,19 +466,16 @@
             jax.ShapeDtypeStruct((3, 3, 27, 64), F32),
             jax.ShapeDtypeStruct((27, 8, 8, 128), F32),
         ),
-        in_specs=[vmem] * 8,
+        in_specs=[vmem] * 9,
         out_specs=(hbm, hbm, vmem),
         input_output_aliases={0: 2},
         scratch_shapes=[
             pltpu.VMEM((5, 5, 32, 128), F32),
             pltpu.VMEM((5, 5, 32, 128), F32),
-            pltpu.VMEM((8, 8, 128), jnp.int32),
-            pltpu.VMEM((3, 8, 8, 128), jnp.int32),
-            pltpu.VMEM((3, 32, 128), jnp.int32),
-            pltpu.VMEM((6, 6, 27, 128), F32),
+            pltpu.VMEM((2, 6, 27, 128), F32),
+            pltpu.VMEM((2, 4, 27, 128), F32),
             pltpu.VMEM((3, 3, 27, 64), F32),
-            pltpu.SemaphoreType.DMA((3,)),
-            pltpu.SemaphoreType.DMA,
+            pltpu.SemaphoreType.DMA((6,)),
         ],
         compiler_params=pltpu.CompilerParams(vmem_limit_bytes=24 * 2**20),
     )(*args)

time: 22.9 us -> 21.8 us (0.952)
  Pallas kernels: 22.2 us -> 21 us
    pallas_call x1, Pallas kernels: 2.88 us -> 1.73 us  [step(): pl.pallas_call(step_kernel, out_shape=(jax.ShapeDtypeStruct((6, 6, 27, 12...]
where the time goes in v3:
time: 21.8 us; the launch traced here: 21.6 us
  Pallas kernels  21 us (96%)
  between operations  0.64 us (3%)
    pallas_call x1, Pallas kernels, exchange(): pl.pallas_call(functools.partial(exchange_kernel, n_stream, n_span), out_...  19.3 us
    pallas_call x1, Pallas kernels, step(): pl.pallas_call(step_kernel, out_shape=(jax.ShapeDtypeStruct((6, 6, 27, 12...  1.73 us

profile of v3, /device:TPU:1, one launch (start us, length us, event | category | flops | bytes accessed | tf_op | source)
XLA Modules:
  0.0 21.6 jit_solution(1752869363545486376)
XLA Ops:
  0.6 19.3 %shard_map.68 = (f32[27,8,8,128]{3,2,1,0:T(8,128)S(1)}, f32[4,64,128]{2,1,0:T(8,128)S(1)}, f32[4,24,128]{2,1,0:T(8,128)S(1)}, f32[3,3,27,128]{3,2,1,0:T(8,128)S(...) custom-call(f32[6,6,27,128]{3,2,1,0:T(8,128)} %bitcast.4, ...), custom_call_target="tpu_custom_call" | custom-call | tf_op jit(solution)/shard_map/pallas_call | solution.py:173
  19.9 1.7 %shard_map.69 = (f32[6,6,27,128]{3,2,1,0:T(8,128)}, f32[3,3,27,64]{3,2,1,0:T(8,128)}, f32[27,8,8,128]{3,2,1,0:T(8,128)S(1)}) custom-call(f32[27,8,8,128]{3,2,1,0:T(8,128)S(1)} %get-tuple-element.13.given, f32[4,64,128]{2,1,0:T(8,128)S(1)} %get-tuple-element.14.faces, f32[4,24,128]{2,1,0:T(8,128)S(1)} %get-tuple-element.15.corners, ...), custom_call_target="tpu_custom_call", output_to_operand_aliasing={{2}: (0, {})} | custom-call | tf_op jit(solution)/shard_map/pallas_call | solution.py:462

commit v4 on v3

--- a/solution.py
+++ b/solution.py
@@ -28,6 +28,11 @@
     return [(1 - dx, j) for j in range(3)] if dx else [(i, 1 - dy) for i in range(3)]
 
 
+def halo_cells(side):
+    dx, dy = side
+    return [(2 + 2 * dx, 1 + j) if dx else (1 + j, 2 + 2 * dy) for j in range(3)]
+
+
 def end_pops(side):
     dx, dy = side
     return [face_pops((0, s) if dx else (s, 0)) for s in (-1, 1)]
@@ -41,10 +46,17 @@
     return [table[n, 0, pl.ds(q, 1), :] for q in range(27)], [table[n, 1, pl.ds(q, 1), :] for q in range(27)]
 
 
+def unfold(raw, tall, fold):
+    raw[pl.ds(0, 16), :] = fold
+    raw[pl.ds(16, 16), :] = pltpu.roll(fold, 64, 1)
+    tall[pl.ds(0, 16), :] = stretch(fold)
+    tall[pl.ds(16, 16), :] = stretch(fold, 1)
+
+
 def exchange_kernel(
     n_stream, n_span, fine, coarse, obstacle, level, rates,
-    turned, faces, corners, tall, own, inner, coarse_stop, table, around,
-    native, flags, levels, speeds, blocked, rolled, face_out, corner_out, load_sem, send_sem, recv_sem,
+    turned, faces, corners, halo, tall, inner, coarse_stop, table, around,
+    native, own, flags, levels, speeds, blocked, rolled, face_out, corner_out, load_sem, send_sem, recv_sem,
 ):
     row, col = lax.axis_index("stream"), lax.axis_index("span")
 
@@ -52,9 +64,12 @@
         return (lax.rem(row + side[0] + n_stream, n_stream), lax.rem(col + side[1] + n_span, n_span))
 
     barrier = pltpu.get_barrier_semaphore()
+    for i in range(3):
+        for j in range(3):
+            own[i, j, pl.ds(24, 8), :] = jnp.zeros((8, 64), F32)
     loads = [
         pltpu.make_async_copy(fine, native, load_sem.at[0]),
-        pltpu.make_async_copy(coarse, own, load_sem.at[1]),
+        pltpu.make_async_copy(coarse, own.at[:, :, pl.ds(0, 27)], load_sem.at[1]),
         pltpu.make_async_copy(level, levels, load_sem.at[2]),
         pltpu.make_async_copy(obstacle, flags, load_sem.at[3]),
         pltpu.make_async_copy(rates, speeds, load_sem.at[4]),
@@ -70,36 +85,37 @@
     for slot, side in enumerate(CORNERS):
         dx, dy = side
         cell = own[1 - dx, 1 - dy]
-        corner_out[slot, pl.ds(0, 14), :] = jnp.concatenate([cell[0:14], cell[13:27]], axis=1)
-        corner_out[slot, pl.ds(14, 3), :] = native[
+        corner_out[slot, pl.ds(0, 16), :] = jnp.concatenate([cell[0:16], cell[16:32]], axis=1)
+        corner_out[slot, pl.ds(16, 3), :] = native[
             5 if dx < 0 else 0, 5 if dy < 0 else 0, pl.ds(corner_start(side), 3), :
         ]
     for slot, side in enumerate(FACES):
         dx, dy = side
         both = (here == 1) & (there[FACES.index((-dx, -dy))] == 1)
         cells = [own[i, j] for i, j in face_cells(side)]
-        face_out[slot, pl.ds(0, 27), :] = jnp.concatenate([cells[0], cells[1]], axis=1)
-        face_out[slot, pl.ds(27, 27), :] = jnp.concatenate([cells[2], cells[2]], axis=1)
+        face_out[slot, pl.ds(0, 32), :] = jnp.concatenate([cells[0], cells[1]], axis=1)
+        face_out[slot, pl.ds(32, 16), :] = jnp.concatenate([cells[2][0:16], cells[2][16:32]], axis=1)
+        face_out[slot, pl.ds(48, 8), :] = jnp.zeros((8, 128), F32)
         edge = native[5 if dx < 0 else 0] if dx else native[:, 5 if dy < 0 else 0]
         edge = jnp.swapaxes(edge, 0, 1)
         for n, q in enumerate(face_pops(side)):
             spot = face_out.at[slot, pl.ds(6 * n, 6)]
             spot[...] = jnp.where(both, edge[q], spot[...])
         ends = [pick_rows(cell, pops) for cell, pops in zip((cells[0], cells[2]), end_pops(side))]
-        face_out[slot, pl.ds(54, 9), :] = jnp.concatenate(ends, axis=1)
+        face_out[slot, pl.ds(56, 9), :] = jnp.concatenate(ends, axis=1)
     pl.semaphore_wait(barrier, 8)
     copies = []
     for slot, (dx, dy) in enumerate(CORNERS):
         copies.append(
             pltpu.make_async_remote_copy(
-                corner_out.at[slot, pl.ds(0, 17)], corners.at[slot, pl.ds(0, 17)],
+                corner_out.at[slot, pl.ds(0, 19)], corners.at[slot, pl.ds(0, 19)],
                 send_sem.at[4 + slot], recv_sem.at[4 + slot], device_id=at((-dx, -dy)), device_id_type=MESH,
             )
         )
     for slot, (dx, dy) in enumerate(FACES):
         copies.append(
             pltpu.make_async_remote_copy(
-                face_out.at[slot, pl.ds(0, 63)], faces.at[slot, pl.ds(0, 63)],
+                face_out.at[slot, pl.ds(0, 65)], faces.at[slot, pl.ds(0, 65)],
                 send_sem.at[slot], recv_sem.at[slot], device_id=at((-dx, -dy)), device_id_type=MESH,
             )
         )
@@ -110,7 +126,8 @@
     for i in range(3):
         for j in range(3):
             cell = own[i, j]
-            tall[i, j] = stretch(jnp.concatenate([cell, cell], axis=1))
+            halo[i + 1, j + 1, :, pl.ds(0, 64)] = cell
+            tall[i + 1, j + 1] = stretch(jnp.concatenate([cell, cell], axis=1))
     for n, value in enumerate([here] + there):
         around[n] = jnp.full((8, 128), value, jnp.int32)
     for load in loads[3:]:
@@ -159,11 +176,27 @@
 
     lax.fori_loop(1, 5, middle, 0)
     for x in range(1, 5):
-        line = [mix(tall[x // 2, j], tall[x // 2 - 1 + 2 * (x % 2), j]) for j in range(3)]
+        line = [mix(tall[x // 2 + 1, j, pl.ds(0, 27), :], tall[x // 2 + 2 * (x % 2), j, pl.ds(0, 27), :]) for j in (1, 2, 3)]
         for y in range(1, 5):
             exploded = mix(line[y // 2], line[y // 2 - 1 + 2 * (y % 2)])
             inner[x - 1, y - 1] = jnp.where(here == 1, inner[x - 1, y - 1], exploded)
-    for copy in copies:
+    for slot, side in enumerate(FACES):
+        copies[4 + slot].wait()
+        pair, fold = faces[slot, pl.ds(0, 32), :], faces[slot, pl.ds(32, 16), :]
+        spots = halo_cells(side)
+        halo[spots[0][0], spots[0][1]] = pair
+        halo[spots[1][0], spots[1][1]] = pltpu.roll(pair, 64, 1)
+        tall[spots[0][0], spots[0][1]] = stretch(pair)
+        tall[spots[1][0], spots[1][1]] = stretch(pair, 1)
+        unfold(halo.at[spots[2][0], spots[2][1]], tall.at[spots[2][0], spots[2][1]], fold)
+        both = (here == 1) & (there[slot] == 1)
+        ends = faces[slot, pl.ds(56, 9), :]
+        for half, (spot, pops) in enumerate(zip((spots[0], spots[2]), end_pops(side))):
+            rows = stretch(ends, half)
+            for n in (0, 3, 6):
+                place = tall.at[spot[0], spot[1], pl.ds(pops[n], 3)]
+                place[...] = jnp.where(both, rows[n : n + 3], place[...])
+    for copy in copies[:4]:
         copy.wait()
 
 
@@ -174,10 +207,10 @@
         functools.partial(exchange_kernel, n_stream, n_span),
         out_shape=(
             jax.ShapeDtypeStruct((27, 8, 8, 128), F32),
-            jax.ShapeDtypeStruct((4, 64, 128), F32),
+            jax.ShapeDtypeStruct((4, 72, 128), F32),
             jax.ShapeDtypeStruct((4, 24, 128), F32),
-            jax.ShapeDtypeStruct((3, 3, 27, 128), F32),
-            jax.ShapeDtypeStruct((3, 3, 27, 64), F32),
+            jax.ShapeDtypeStruct((5, 5, 32, 128), F32),
+            jax.ShapeDtypeStruct((5, 5, 32, 128), F32),
             jax.ShapeDtypeStruct((4, 4, 27, 128), F32),
             jax.ShapeDtypeStruct((3, 32, 128), jnp.int32),
             jax.ShapeDtypeStruct((2, 2, 32, 128), F32),
@@ -187,12 +220,13 @@
         out_specs=(vmem,) * 9,
         scratch_shapes=[
             pltpu.VMEM((6, 6, 27, 128), F32),
+            pltpu.VMEM((3, 3, 32, 64), F32),
             pltpu.VMEM((6, 6, 128), jnp.int32),
             pltpu.SMEM((16, 32), jnp.int32),
             pltpu.SMEM((27,), F32),
             pltpu.VMEM((8, 8, 128), jnp.int32),
             pltpu.VMEM((3, 8, 8, 128), jnp.int32),
-            pltpu.VMEM((4, 64, 128), F32),
+            pltpu.VMEM((4, 72, 128), F32),
             pltpu.VMEM((4, 24, 128), F32),
             pltpu.SemaphoreType.DMA((5,)),
             pltpu.SemaphoreType.DMA((8,)),
@@ -256,14 +290,14 @@
 
 
 def take(values, index):
-    return jnp.take_along_axis(values, index, axis=1)
-
-
-def stretch(values):
+    return jnp.take_along_axis(values, index, axis=1, mode="promise_in_bounds")
+
+
+def stretch(values, half=0):
     at = lane(values.shape)
     middle = lax.shift_right_logical(at, 1)
     beside = jnp.clip(middle + 2 * (at & 1) - 1, 0, 63)
-    return 0.75 * take(values, middle) + 0.25 * take(values, beside)
+    return 0.75 * take(values, middle + 64 * half) + 0.25 * take(values, beside + 64 * half)
 
 
 def shrink(values):
@@ -277,8 +311,8 @@
 
 
 def step_kernel(
-    given, faces, corners, own_tall, own, inner, coarse_stop, table, around, fine_next, coarse_next, turned,
-    halo, tall, edge_x, edge_y, coarse_out, sems,
+    given, faces, corners, halo, tall, inner, coarse_stop, table, around, fine_next, coarse_next, turned,
+    corner_raw, corner_tall, edge_x, edge_y, coarse_out, sems,
 ):
     inner_copy = pltpu.make_async_copy(inner, fine_next.at[pl.ds(1, 4), pl.ds(1, 4)], sems.at[0])
     inner_copy.start()
@@ -299,49 +333,16 @@
         return inner[x - 1, y - 1]
 
     refined = jnp.max(around[0]) == 1
-
-    def halo_cells(side):
-        dx, dy = side
-        return [(2 + 2 * dx, 1 + j) if dx else (1 + j, 2 + 2 * dy) for j in range(3)]
-
-    def received(raw):
-        for slot, (dx, dy) in enumerate(CORNERS):
-            both = corners[slot, pl.ds(0, 14), :]
-            other = pltpu.roll(both, 64, 1)
-            if raw:
-                halo[2 + 2 * dx, 2 + 2 * dy, pl.ds(13, 14), :] = other
-                halo[2 + 2 * dx, 2 + 2 * dy, pl.ds(0, 14), :] = both
-            tall[2 + 2 * dx, 2 + 2 * dy, pl.ds(13, 14), :] = stretch(other)
-            tall[2 + 2 * dx, 2 + 2 * dy, pl.ds(0, 14), :] = stretch(both)
-        for slot, side in enumerate(FACES):
-            spots = halo_cells(side)
-            pair = faces[slot, pl.ds(0, 27), :]
-            for spot, cell in zip(spots, (pair, pltpu.roll(pair, 64, 1), faces[slot, pl.ds(27, 27), :])):
-                if raw:
-                    halo[spot[0], spot[1], pl.ds(0, 27), :] = cell
-                tall[spot[0], spot[1], pl.ds(0, 27), :] = stretch(cell)
-        for i in range(3):
-            for j in range(3):
-                if raw:
-                    halo[i + 1, j + 1, pl.ds(0, 27), pl.ds(0, 64)] = own[i, j]
+    for slot in range(4):
+        unfold(corner_raw.at[slot], corner_tall.at[slot], corners[slot, pl.ds(0, 16), :])
 
     def tall_at(i, j, start, count):
-        if 0 < i < 4 and 0 < j < 4:
-            return own_tall[i - 1, j - 1, pl.ds(start, count), :]
+        if i % 4 == 0 and j % 4 == 0:
+            return corner_tall[i // 4 * 2 + j // 4, pl.ds(start, count), :]
         return tall[i, j, pl.ds(start, count), :]
 
     @pl.when(refined)
     def _():
-        received(False)
-        for slot, side in enumerate(FACES):
-            ends = faces[slot, pl.ds(54, 9), :]
-            spots = halo_cells(side)
-            take_ends = level(1 + slot, 1)
-            for spot, pops, rows in zip((spots[0], spots[2]), end_pops(side), (ends, pltpu.roll(ends, 64, 1))):
-                rows = stretch(rows)
-                for n in (0, 3, 6):
-                    place = tall.at[spot[0], spot[1], pl.ds(pops[n], 3)]
-                    place[...] = jnp.where(take_ends, rows[n : n + 3], place[...])
         for slot, side in enumerate(FACES):
             dx, dy = side
             pops = face_pops(side)
@@ -372,7 +373,7 @@
                 mix(tall_at(ei, ej, start, 3), tall_at(ii, ej, start, 3)),
                 mix(tall_at(ei, ij, start, 3), tall_at(ii, ij, start, 3)),
             )
-            value = jnp.where(level(5 + slot, 3), corners[slot, pl.ds(14, 3), :], exploded)
+            value = jnp.where(level(5 + slot, 3), corners[slot, pl.ds(16, 3), :], exploded)
             for c in range(3):
                 turned[start + c, 7 if dx > 0 else 0, pl.ds(7 if dy > 0 else 0, 1), :] = value[c : c + 1]
 
@@ -412,7 +413,6 @@
 
     @pl.when(jnp.logical_not(refined))
     def _():
-        received(True)
         for x in range(6):
             line = [mix(tall_at(x // 2 + 1, j, 0, 27), tall_at(x // 2 + 2 * (x % 2), j, 0, 27)) for j in range(5)]
             for y in range(6) if x % 5 == 0 else (0, 5):
@@ -429,7 +429,12 @@
         keep, pull = rates_of(table, 1)
         flat = turned.reshape(27 * 64, 128)
         for i in range(5):
-            cells = jnp.swapaxes(halo[i, :, pl.ds(0, 27), :], 0, 1)
+            if i % 4 == 0:
+                ends = [corner_raw[i // 4 * 2 + n, pl.ds(0, 27), :] for n in range(2)]
+                cells = jnp.stack([ends[0]] + [halo[i, j, pl.ds(0, 27), :] for j in (1, 2, 3)] + [ends[1]])
+            else:
+                cells = halo[i, :, pl.ds(0, 27), :]
+            cells = jnp.swapaxes(cells, 0, 1)
             for q in range(27):
                 flat[pl.ds(64 * q + 5 * i, 5), :] = cells[q]
         g = []
@@ -470,8 +475,8 @@
         out_specs=(hbm, hbm, vmem),
         input_output_aliases={0: 2},
         scratch_shapes=[
-            pltpu.VMEM((5, 5, 32, 128), F32),
-            pltpu.VMEM((5, 5, 32, 128), F32),
+            pltpu.VMEM((4, 32, 128), F32),
+            pltpu.VMEM((4, 32, 128), F32),
             pltpu.VMEM((2, 6, 27, 128), F32),
             pltpu.VMEM((2, 4, 27, 128), F32),
             pltpu.VMEM((3, 3, 27, 64), F32),

time: 21.8 us -> 21.7 us (level)
  no operation moved by 1% of the time
where the time goes in v4:
time: 21.7 us
  Pallas kernels  21.1 us (97%)
  between operations  0.64 us (3%)
    pallas_call x1, Pallas kernels, exchange(): pl.pallas_call(functools.partial(exchange_kernel, n_stream, n_span), out_...  19.5 us
    pallas_call x1, Pallas kernels, step(): pl.pallas_call(step_kernel, out_shape=(jax.ShapeDtypeStruct((6, 6, 27, 12...  1.63 us

profile of v4, /device:TPU:1, one launch (start us, length us, event | category | flops | bytes accessed | tf_op | source)
XLA Modules:
  0.0 21.7 jit_solution(4184671612352919918)
XLA Ops:
  0.6 19.5 %shard_map.68 = (f32[27,8,8,128]{3,2,1,0:T(8,128)S(1)}, f32[4,72,128]{2,1,0:T(8,128)S(1)}, f32[4,24,128]{2,1,0:T(8,128)S(1)}, f32[5,5,32,128]{3,2,1,0:T(8,128)S(...) custom-call(f32[6,6,27,128]{3,2,1,0:T(8,128)} %bitcast.4, ...), custom_call_target="tpu_custom_call" | custom-call | tf_op jit(solution)/shard_map/pallas_call | solution.py:206
  20.1 1.6 %shard_map.69 = (f32[6,6,27,128]{3,2,1,0:T(8,128)}, f32[3,3,27,64]{3,2,1,0:T(8,128)}, f32[27,8,8,128]{3,2,1,0:T(8,128)S(1)}) custom-call(f32[27,8,8,128]{3,2,1,0:T(8,128)S(1)} %get-tuple-element.13.given, f32[4,72,128]{2,1,0:T(8,128)S(1)} %get-tuple-element.14.faces, f32[4,24,128]{2,1,0:T(8,128)S(1)} %get-tuple-element.15.corners, ...), custom_call_target="tpu_custom_call", output_to_operand_aliasing={{2}: (0, {})} | custom-call | tf_op jit(solution)/shard_map/pallas_call | solution.py:467

commit v5 on v4

--- a/solution.py
+++ b/solution.py
@@ -55,8 +55,8 @@
 
 def exchange_kernel(
     n_stream, n_span, fine, coarse, obstacle, level, rates,
-    turned, faces, corners, halo, tall, inner, coarse_stop, table, around,
-    native, own, flags, levels, speeds, blocked, rolled, face_out, corner_out, load_sem, send_sem, recv_sem,
+    turned, faces, corners, ends_raw, tall, grid, inner, coarse_stop, table, around,
+    halo, native, own, flags, levels, speeds, blocked, rolled, face_out, corner_out, load_sem, send_sem, recv_sem,
 ):
     row, col = lax.axis_index("stream"), lax.axis_index("span")
 
@@ -64,6 +64,8 @@
         return (lax.rem(row + side[0] + n_stream, n_stream), lax.rem(col + side[1] + n_span, n_span))
 
     barrier = pltpu.get_barrier_semaphore()
+    for side in CORNERS + FACES:
+        pl.semaphore_signal(barrier, inc=1, device_id=at(side), device_id_type=MESH)
     for i in range(3):
         for j in range(3):
             own[i, j, pl.ds(24, 8), :] = jnp.zeros((8, 64), F32)
@@ -76,8 +78,6 @@
     ]
     for load in loads:
         load.start()
-    for side in CORNERS + FACES:
-        pl.semaphore_signal(barrier, inc=1, device_id=at(side), device_id_type=MESH)
     for load in loads[:3]:
         load.wait()
     here = levels[row, col]
@@ -196,6 +196,13 @@
             for n in (0, 3, 6):
                 place = tall.at[spot[0], spot[1], pl.ds(pops[n], 3)]
                 place[...] = jnp.where(both, rows[n : n + 3], place[...])
+    for i in (1, 2, 3):
+        cells = jnp.swapaxes(halo[i, :, pl.ds(0, 27), :], 0, 1)
+        for q in range(27):
+            grid[q, pl.ds(5 * i, 5), :] = cells[q]
+    for n, i in enumerate((0, 4)):
+        for j in (1, 2, 3):
+            ends_raw[n, j] = halo[i, j]
     for copy in copies[:4]:
         copy.wait()
 
@@ -209,16 +216,18 @@
             jax.ShapeDtypeStruct((27, 8, 8, 128), F32),
             jax.ShapeDtypeStruct((4, 72, 128), F32),
             jax.ShapeDtypeStruct((4, 24, 128), F32),
+            jax.ShapeDtypeStruct((2, 5, 32, 128), F32),
             jax.ShapeDtypeStruct((5, 5, 32, 128), F32),
-            jax.ShapeDtypeStruct((5, 5, 32, 128), F32),
+            jax.ShapeDtypeStruct((27, 32, 128), F32),
             jax.ShapeDtypeStruct((4, 4, 27, 128), F32),
             jax.ShapeDtypeStruct((3, 32, 128), jnp.int32),
             jax.ShapeDtypeStruct((2, 2, 32, 128), F32),
             jax.ShapeDtypeStruct((9, 8, 128), jnp.int32),
         ),
         in_specs=[hbm] * 5,
-        out_specs=(vmem,) * 9,
+        out_specs=(vmem,) * 10,
         scratch_shapes=[
+            pltpu.VMEM((5, 5, 32, 128), F32),
             pltpu.VMEM((6, 6, 27, 128), F32),
             pltpu.VMEM((3, 3, 32, 64), F32),
             pltpu.VMEM((6, 6, 128), jnp.int32),
@@ -311,7 +320,8 @@
 
 
 def step_kernel(
-    given, faces, corners, halo, tall, inner, coarse_stop, table, around, fine_next, coarse_next, turned,
+    given, faces, corners, ends_raw, tall, middle, inner, coarse_stop, table, around,
+    fine_next, coarse_next, turned, grid,
     corner_raw, corner_tall, edge_x, edge_y, coarse_out, sems,
 ):
     inner_copy = pltpu.make_async_copy(inner, fine_next.at[pl.ds(1, 4), pl.ds(1, 4)], sems.at[0])
@@ -427,30 +437,26 @@
             y_copies[n].start()
 
         keep, pull = rates_of(table, 1)
-        flat = turned.reshape(27 * 64, 128)
-        for i in range(5):
-            if i % 4 == 0:
-                ends = [corner_raw[i // 4 * 2 + n, pl.ds(0, 27), :] for n in range(2)]
-                cells = jnp.stack([ends[0]] + [halo[i, j, pl.ds(0, 27), :] for j in (1, 2, 3)] + [ends[1]])
-            else:
-                cells = halo[i, :, pl.ds(0, 27), :]
-            cells = jnp.swapaxes(cells, 0, 1)
+        for n in range(2):
+            cells = [ends_raw[n, j, pl.ds(0, 27), :] for j in (1, 2, 3)]
+            cells = [corner_raw[2 * n, pl.ds(0, 27), :]] + cells + [corner_raw[2 * n + 1, pl.ds(0, 27), :]]
+            cells = jnp.swapaxes(jnp.stack(cells), 0, 1)
             for q in range(27):
-                flat[pl.ds(64 * q + 5 * i, 5), :] = cells[q]
+                grid[q, pl.ds(20 * n, 5), :] = cells[q]
         g = []
         for q in range(27):
             ex, ey, ez = q // 9 - 1, q // 3 % 3 - 1, q % 3 - 1
             start = 6 - 5 * ex - ey
-            source = flat[pl.ds(64 * q + start, 13), :]
+            source = grid[q, pl.ds(start, 13), :]
             if ez:
                 source = pltpu.roll(source, ez % 128, 1)
             if q != 13:
                 stop = coarse_stop[ez + 1, pl.ds(start, 13), :]
-                source = jnp.where(stop != 0, flat[pl.ds(64 * (26 - q) + 6, 13), :], source)
+                source = jnp.where(stop != 0, grid[26 - q, pl.ds(6, 13), :], source)
             g.append(source)
         new = collide(g, keep, pull)
         wall = coarse_stop[1, pl.ds(6, 13), :] != 0
-        new = [jnp.where(wall, flat[pl.ds(64 * q + 6, 13), :], new[q]) for q in range(27)]
+        new = [jnp.where(wall, grid[q, pl.ds(6, 13), :], new[q]) for q in range(27)]
         turn = jnp.swapaxes(jnp.stack(new), 0, 1)
         for i in range(3):
             for j in range(3):
@@ -470,10 +476,11 @@
             jax.ShapeDtypeStruct((6, 6, 27, 128), F32),
             jax.ShapeDtypeStruct((3, 3, 27, 64), F32),
             jax.ShapeDtypeStruct((27, 8, 8, 128), F32),
+            jax.ShapeDtypeStruct((27, 32, 128), F32),
         ),
-        in_specs=[vmem] * 9,
-        out_specs=(hbm, hbm, vmem),
-        input_output_aliases={0: 2},
+        in_specs=[vmem] * 10,
+        out_specs=(hbm, hbm, vmem, vmem),
+        input_output_aliases={0: 2, 5: 3},
         scratch_shapes=[
             pltpu.VMEM((4, 32, 128), F32),
             pltpu.VMEM((4, 32, 128), F32),
@@ -493,7 +500,7 @@
         fine = jnp.transpose(fine_pops, (1, 2, 0, 3))
         coarse = jnp.transpose(coarse_pops, (1, 2, 0, 3))
         ready = exchange(n_stream, n_span, fine, coarse, obstacle, block_level, relax_rates)
-        fine_next, coarse_next, _ = step(*ready)
+        fine_next, coarse_next, *_ = step(*ready)
         return jnp.transpose(fine_next, (2, 0, 1, 3)), jnp.transpose(coarse_next, (2, 0, 1, 3))
 
     placed = P(None, "stream", "span", None)

time: 21.7 us -> 21.7 us (level)
  no operation moved by 1% of the time
where the time goes in v5:
time: 21.7 us
  Pallas kernels  21.1 us (97%)
  between operations  0.64 us (3%)
    pallas_call x1, Pallas kernels, exchange(): pl.pallas_call(functools.partial(exchange_kernel, n_stream, n_span), out_...  19.5 us
    pallas_call x1, Pallas kernels, step(): pl.pallas_call(step_kernel, out_shape=(jax.ShapeDtypeStruct((6, 6, 27, 12...  1.63 us

profile of v5, /device:TPU:1, one launch (start us, length us, event | category | flops | bytes accessed | tf_op | source)
XLA Modules:
  0.0 21.7 jit_solution(14317894213292182765)
XLA Ops:
  0.6 19.5 %shard_map.68 = (f32[27,8,8,128]{3,2,1,0:T(8,128)S(1)}, f32[4,72,128]{2,1,0:T(8,128)S(1)}, f32[4,24,128]{2,1,0:T(8,128)S(1)}, f32[2,5,32,128]{3,2,1,0:T(8,128)S(...) custom-call(f32[6,6,27,128]{3,2,1,0:T(8,128)} %bitcast.4, ...), custom_call_target="tpu_custom_call" | custom-call | tf_op jit(solution)/shard_map/pallas_call | solution.py:213
  20.1 1.6 %shard_map.69 = (f32[6,6,27,128]{3,2,1,0:T(8,128)}, f32[3,3,27,64]{3,2,1,0:T(8,128)}, f32[27,8,8,128]{3,2,1,0:T(8,128)S(1)}, f32[27,32,128]{2,1,0:T(8,128)S(1)}) custom-call(f32[27,8,8,128]{3,2,1,0:T(8,128)S(1)} %get-tuple-element.14.given, f32[4,72,128]{2,1,0:T(8,128)S(1)} %get-tuple-element.15.faces, ...), custom_call_target="tpu_custom_call", output_to_operand_aliasing={{2}: (0, {}), {3}: (5, {})} | custom-call | tf_op jit(solution)/shard_map/pallas_call | solution.py:473

commit v6 on v5

--- a/solution.py
+++ b/solution.py
@@ -55,7 +55,7 @@
 
 def exchange_kernel(
     n_stream, n_span, fine, coarse, obstacle, level, rates,
-    turned, faces, corners, ends_raw, tall, grid, inner, coarse_stop, table, around,
+    turned, faces, corners, ends_raw, tall, grid, inner, sums, coarse_stop, table, around,
     halo, native, own, flags, levels, speeds, blocked, rolled, face_out, corner_out, load_sem, send_sem, recv_sem,
 ):
     row, col = lax.axis_index("stream"), lax.axis_index("span")
@@ -180,29 +180,30 @@
         for y in range(1, 5):
             exploded = mix(line[y // 2], line[y // 2 - 1 + 2 * (y % 2)])
             inner[x - 1, y - 1] = jnp.where(here == 1, inner[x - 1, y - 1], exploded)
+    for i in range(3):
+        for j in range(3):
+            xs = [x for x in (2 * i, 2 * i + 1) if x % 5]
+            parts = [inner[x - 1, y - 1] for x in xs for y in (2 * j, 2 * j + 1) if y % 5]
+            sums[i, j] = functools.reduce(jnp.add, parts)
     for slot, side in enumerate(FACES):
         copies[4 + slot].wait()
         pair, fold = faces[slot, pl.ds(0, 32), :], faces[slot, pl.ds(32, 16), :]
         spots = halo_cells(side)
-        halo[spots[0][0], spots[0][1]] = pair
-        halo[spots[1][0], spots[1][1]] = pltpu.roll(pair, 64, 1)
+        raw = [ends_raw.at[i // 4, j] if i % 4 == 0 else halo.at[i, j] for i, j in spots]
+        raw[0][...] = pair
+        raw[1][...] = pltpu.roll(pair, 64, 1)
         tall[spots[0][0], spots[0][1]] = stretch(pair)
         tall[spots[1][0], spots[1][1]] = stretch(pair, 1)
-        unfold(halo.at[spots[2][0], spots[2][1]], tall.at[spots[2][0], spots[2][1]], fold)
-        both = (here == 1) & (there[slot] == 1)
+        unfold(raw[2], tall.at[spots[2][0], spots[2][1]], fold)
         ends = faces[slot, pl.ds(56, 9), :]
         for half, (spot, pops) in enumerate(zip((spots[0], spots[2]), end_pops(side))):
             rows = stretch(ends, half)
             for n in (0, 3, 6):
-                place = tall.at[spot[0], spot[1], pl.ds(pops[n], 3)]
-                place[...] = jnp.where(both, rows[n : n + 3], place[...])
+                tall[spot[0], spot[1], pl.ds(pops[n], 3), :] = rows[n : n + 3]
     for i in (1, 2, 3):
         cells = jnp.swapaxes(halo[i, :, pl.ds(0, 27), :], 0, 1)
         for q in range(27):
             grid[q, pl.ds(5 * i, 5), :] = cells[q]
-    for n, i in enumerate((0, 4)):
-        for j in (1, 2, 3):
-            ends_raw[n, j] = halo[i, j]
     for copy in copies[:4]:
         copy.wait()
 
@@ -220,12 +221,13 @@
             jax.ShapeDtypeStruct((5, 5, 32, 128), F32),
             jax.ShapeDtypeStruct((27, 32, 128), F32),
             jax.ShapeDtypeStruct((4, 4, 27, 128), F32),
+            jax.ShapeDtypeStruct((3, 3, 27, 128), F32),
             jax.ShapeDtypeStruct((3, 32, 128), jnp.int32),
             jax.ShapeDtypeStruct((2, 2, 32, 128), F32),
             jax.ShapeDtypeStruct((9, 8, 128), jnp.int32),
         ),
         in_specs=[hbm] * 5,
-        out_specs=(vmem,) * 10,
+        out_specs=(vmem,) * 11,
         scratch_shapes=[
             pltpu.VMEM((5, 5, 32, 128), F32),
             pltpu.VMEM((6, 6, 27, 128), F32),
@@ -320,7 +322,7 @@
 
 
 def step_kernel(
-    given, faces, corners, ends_raw, tall, middle, inner, coarse_stop, table, around,
+    given, faces, corners, ends_raw, tall, middle, inner, sums, coarse_stop, table, around,
     fine_next, coarse_next, turned, grid,
     corner_raw, corner_tall, edge_x, edge_y, coarse_out, sems,
 ):
@@ -338,9 +340,7 @@
     def cell(x, y):
         if x % 5 == 0:
             return edge_x[x // 5, y]
-        if y % 5 == 0:
-            return edge_y[y // 5, x - 1]
-        return inner[x - 1, y - 1]
+        return edge_y[y // 5, x - 1]
 
     refined = jnp.max(around[0]) == 1
     for slot in range(4):
@@ -415,9 +415,11 @@
             y_copies[n].start()
         for i in range(3):
             for j in range(3):
-                total = (cell(2 * i, 2 * j) + cell(2 * i, 2 * j + 1)) + (
-                    cell(2 * i + 1, 2 * j) + cell(2 * i + 1, 2 * j + 1)
-                )
+                spots = [(x, y) for x in (2 * i, 2 * i + 1) for y in (2 * j, 2 * j + 1)]
+                total = sums[i, j]
+                for x, y in spots:
+                    if x % 5 == 0 or y % 5 == 0:
+                        total = total + cell(x, y)
                 coarse_out[i, j] = shrink(total)[:, :64]
         coarse_copy.start()
 
@@ -478,7 +480,7 @@
             jax.ShapeDtypeStruct((27, 8, 8, 128), F32),
             jax.ShapeDtypeStruct((27, 32, 128), F32),
         ),
-        in_specs=[vmem] * 10,
+        in_specs=[vmem] * 11,
         out_specs=(hbm, hbm, vmem, vmem),
         input_output_aliases={0: 2, 5: 3},
         scratch_shapes=[

time: 21.7 us -> 21.7 us (level); the launches traced: 21.7 us -> 21.5 us
  Pallas kernels: 21.1 us -> 20.8 us
    pallas_call x1, Pallas kernels: 1.63 us -> 1.35 us  [step(): pl.pallas_call(step_kernel, out_shape=(jax.ShapeDtypeStruct((6, 6, 27, 12...]
where the time goes in v6:
time: 21.7 us; the launch traced here: 21.5 us
  Pallas kernels  20.8 us (96%)
  between operations  0.64 us (3%)
    pallas_call x1, Pallas kernels, exchange(): pl.pallas_call(functools.partial(exchange_kernel, n_stream, n_span), out_...  19.5 us
    pallas_call x1, Pallas kernels, step(): pl.pallas_call(step_kernel, out_shape=(jax.ShapeDtypeStruct((6, 6, 27, 12...  1.35 us

profile of v6, /device:TPU:1, one launch (start us, length us, event | category | flops | bytes accessed | tf_op | source)
XLA Modules:
  0.0 21.5 jit_solution(16780495548451973651)
XLA Ops:
  0.6 19.5 %shard_map.68 = (f32[27,8,8,128]{3,2,1,0:T(8,128)S(1)}, f32[4,72,128]{2,1,0:T(8,128)S(1)}, f32[4,24,128]{2,1,0:T(8,128)S(1)}, f32[2,5,32,128]{3,2,1,0:T(8,128)S(...) custom-call(f32[6,6,27,128]{3,2,1,0:T(8,128)} %bitcast.4, ...), custom_call_target="tpu_custom_call" | custom-call | tf_op jit(solution)/shard_map/pallas_call | solution.py:214
  20.1 1.4 %shard_map.69 = (f32[6,6,27,128]{3,2,1,0:T(8,128)}, f32[3,3,27,64]{3,2,1,0:T(8,128)}, f32[27,8,8,128]{3,2,1,0:T(8,128)S(1)}, f32[27,32,128]{2,1,0:T(8,128)S(1)}) custom-call(f32[27,8,8,128]{3,2,1,0:T(8,128)S(1)} %get-tuple-element.15.given, f32[4,72,128]{2,1,0:T(8,128)S(1)} %get-tuple-element.16.faces, ...), custom_call_target="tpu_custom_call", output_to_operand_aliasing={{2}: (0, {}), {3}: (5, {})} | custom-call | tf_op jit(solution)/shard_map/pallas_call | solution.py:475
